TPU v7x, 256 devices: a whole 4x4x8 slice. The times are simulated.
256 devices in a mesh: gx: 16 (over x, z_hi, core), gy: 4 (over y), gz: 4 (over z_lo).
Axes of the slice: x: 4, y: 4, z: 8 (z_hi: 2, z_lo: 4; z = z_hi * 4 + z_lo), core: 2. Of those that a mesh axis runs over, the one named last changes fastest.
Arguments:
- populations: float32 [19, 128, 32, 512], P(None, 'gx', 'gy', 'gz'), may hold values from 0 to 1, as said below
- adjoint_seed: float32 [19, 128, 32, 512], P(None, 'gx', 'gy', 'gz'), may hold values from -6 to 6
- wall_slip: float32 [128, 32, 512], P('gx', 'gy', 'gz'), may hold values from 0.1 to 0.9
- permeability: float32 [128, 32, 512], P('gx', 'gy', 'gz'), may hold values from 0.2 to 0.95
- cell_kinds: int32 [128, 32, 512], P('gx', 'gy', 'gz'), may hold values from 0 to 2
Outputs:
- grad_populations: float32 [19, 128, 32, 512], P(None, 'gx', 'gy', 'gz')
- grad_slip: float32 [128, 32, 512], P('gx', 'gy', 'gz')
- grad_permeability: float32 [128, 32, 512], P('gx', 'gy', 'gz')
Inputs may be any that keep to these rules, and one draw needn't show every extreme that they name: `populations`: each population is its lattice weight times a factor between 0.25 and 1.75.
All inputs are finite; a program needn't handle non-finite values.
Results may differ from a plain program's by a relative error of at most 0.0003.
Values sent between devices are 32-bit elements; how exact they have to be, the bound alone decides.
A program may use at most 64 MiB of HBM per device.

v0:
```python
import jax
import jax.numpy as jnp
from jax import lax
from jax.experimental import pallas as pl
from jax.experimental.pallas import tpu as pltpu
from jax.sharding import PartitionSpec as P

MESH = pl.DeviceIdType.MESH
VELOCITY = (
    (0, 0, 0), (1, 0, 0), (-1, 0, 0), (0, 1, 0), (0, -1, 0), (0, 0, 1), (0, 0, -1),
    (1, 1, 0), (-1, -1, 0), (1, -1, 0), (-1, 1, 0), (1, 0, 1), (-1, 0, -1),
    (1, 0, -1), (-1, 0, 1), (0, 1, 1), (0, -1, -1), (0, 1, -1), (0, -1, 1),
)
OPPOSITE = (0, 2, 1, 4, 3, 6, 5, 8, 7, 10, 9, 12, 11, 14, 13, 16, 15, 18, 17)
ORDER = (1, 7, 9, 11, 13, 2, 8, 10, 12, 14, 3, 4, 5, 6, 15, 16, 17, 18, 0)
SLOT = {v: s for s, v in enumerate(ORDER)}
ALONG_Y = ((3, 7, 10, 15, 17), (4, 8, 9, 16, 18))
ALONG_Z = ((5, 11, 14, 15, 18), (6, 12, 13, 16, 17))
W0, W1, W2 = 1.0 / 3.0, 1.0 / 18.0, 1.0 / 36.0
X, Y, Z = 8, 8, 128
BASE = 16
ROWS = 96


def lane_of(k, x):
    return 16 * k + x + 1


def pairs_of(f):
    plus = {i: f[i] + f[i + 1] for i in range(1, 19, 2)}
    minus = {i: f[i] - f[i + 1] for i in range(1, 19, 2)}
    return plus, minus


def vector_of(m):
    return (
        m[1] + ((m[7] + m[9]) + (m[11] + m[13])),
        m[3] + ((m[7] - m[9]) + (m[15] + m[17])),
        m[5] + ((m[11] - m[13]) + (m[15] - m[17])),
    )


def along(i, u):
    total = None
    for c, part in zip(VELOCITY[i], u):
        if c:
            part = part if c > 0 else -part
            total = part if total is None else total + part
    return total


def macroscopic(f, damping):
    plus, minus = pairs_of(f)
    rho = f[0]
    diagonal = (plus[7] + plus[9]) + (plus[11] + plus[13]) + (plus[15] + plus[17])
    rho = rho + ((plus[1] + plus[3]) + (plus[5] + diagonal))
    m = vector_of(minus)
    k = damping / rho
    u = tuple(part * k for part in m)
    usq = u[0] * u[0] + u[1] * u[1] + u[2] * u[2]
    return plus, minus, rho, m, u, usq


def coefficients(slip, perm, kind):
    wall = kind == 2
    keep = jnp.where(wall, slip, 1.0)
    bounce = jnp.where(wall, 1.0 - slip, 0.0)
    damping = jnp.where(kind == 1, perm, 1.0)
    even = 0.5 * bounce - 0.125 * keep
    odd = -0.5 * bounce - 0.125 * keep
    return keep, damping, even, odd


def collide(f, slip, perm, kind):
    keep, damping, even, odd = coefficients(slip, perm, kind)
    plus, minus, rho, m, u, usq = macroscopic(f, damping)
    scale = 1.25 * keep * rho
    base = 1.0 - 1.5 * usq
    out = {0: 2.0 * even * f[0] + W0 * scale * base}
    s1, s2 = W1 * scale, W2 * scale
    s1_base, s2_base = s1 * base, s2 * base
    for i in range(1, 19, 2):
        s, sb = (s1, s1_base) if i < 7 else (s2, s2_base)
        p = along(i, u)
        sp = s * p
        e = sb + 4.5 * (sp * p) + even * plus[i]
        o = 3.0 * sp + odd * minus[i]
        out[i] = e + o
        out[i + 1] = e - o
    return out


def pull(f, g, slip, perm, kind):
    keep, damping, even, odd = coefficients(slip, perm, kind)
    plus, minus, rho, m, u, usq = macroscopic(f, damping)
    gp, gm = pairs_of(g)
    w1g = {i: W1 * gp[i] for i in (1, 3, 5)}
    s_xy, s_xz, s_yz = gp[7] + gp[9], gp[11] + gp[13], gp[15] + gp[17]
    a0 = W0 * g[0] + W1 * (gp[1] + gp[3] + gp[5]) + W2 * (s_xy + s_xz + s_yz)
    b = (
        W1 * gm[1] + W2 * ((gm[7] + gm[9]) + (gm[11] + gm[13])),
        W1 * gm[3] + W2 * ((gm[7] - gm[9]) + (gm[15] + gm[17])),
        W1 * gm[5] + W2 * ((gm[11] - gm[13]) + (gm[15] - gm[17])),
    )
    dxx = w1g[1] + W2 * (s_xy + s_xz)
    dyy = w1g[3] + W2 * (s_xy + s_yz)
    dzz = w1g[5] + W2 * (s_xz + s_yz)
    dxy, dxz, dyz = W2 * (gp[7] - gp[9]), W2 * (gp[11] - gp[13]), W2 * (gp[15] - gp[17])
    du = (
        dxx * u[0] + dxy * u[1] + dxz * u[2],
        dxy * u[0] + dyy * u[1] + dyz * u[2],
        dxz * u[0] + dyz * u[1] + dzz * u[2],
    )
    udu = u[0] * du[0] + u[1] * du[1] + u[2] * du[2]
    ub = u[0] * b[0] + u[1] * b[1] + u[2] * b[2]
    v = tuple(b[i] + 3.0 * du[i] - a0 * u[i] for i in range(3))
    a0usq = a0 * usq
    g_rho = 1.25 * keep * (a0 + 1.5 * a0usq - 4.5 * udu)
    factor = 3.75 * keep * damping
    g_m = tuple(factor * part for part in v)
    out = {0: 2.0 * even * g[0] + g_rho}
    sum_plus, sum_minus = None, None
    for i in range(1, 19, 2):
        s = even * gp[i] + g_rho
        t = odd * gm[i] + along(i, g_m)
        out[i] = s + t
        out[i + 1] = s - t
        a, c = gp[i] * plus[i], gm[i] * minus[i]
        sum_plus = a if sum_plus is None else sum_plus + a
        sum_minus = c if sum_minus is None else sum_minus + c
    of_wall = (
        0.375 * sum_minus
        - 0.625 * sum_plus
        - 1.25 * (g[0] * f[0])
        + 1.25 * rho * (a0 - 1.5 * a0usq + 3.0 * ub + 4.5 * udu)
    )
    of_porous = 3.75 * (v[0] * m[0] + v[1] * m[1] + v[2] * m[2])
    return out, jnp.where(kind == 2, of_wall, 0.0), jnp.where(kind == 1, of_porous, 0.0)


def kernel(
    pop_hbm, seed_hbm, slip_hbm, perm_hbm, kind_hbm,
    gpop_hbm, gslip_hbm, gperm_hbm,
    pops, out, slip, perm, kind, gslip, gperm, fields, ysend, zsend, yrecv, zrecv,
    load_sem, store_sem, send_sem, recv_sem,
):
    here = tuple(lax.axis_index(a) for a in ("gx", "gy", "gz"))
    sizes = tuple(lax.axis_size(a) for a in ("gx", "gy", "gz"))

    def device(*steps):
        return tuple(
            lax.rem(h + (s + n), n) if s else h for h, s, n in zip(here, steps, sizes)
        )

    neighbours = [c for c in VELOCITY if any(c)]
    col, seed, grad = 0, 1, 2

    load_seed = [
        pltpu.make_async_copy(
            seed_hbm.at[i],
            fields.at[seed, SLOT[OPPOSITE[i]], pl.ds(BASE, X * Y), :],
            load_sem.at[i],
        )
        for i in range(19)
    ]
    for c in load_seed:
        c.start()
    load_rest = [
        pltpu.make_async_copy(src, dst, load_sem.at[19 + n])
        for n, (src, dst) in enumerate(
            ((pop_hbm, pops), (slip_hbm, slip), (perm_hbm, perm), (kind_hbm, kind))
        )
    ]
    for c in load_rest:
        c.start()

    barrier = pltpu.get_barrier_semaphore()
    for c in neighbours:
        pl.semaphore_signal(barrier, inc=1, device_id=device(*c), device_id_type=MESH)

    lane = lax.broadcasted_iota(jnp.int32, (Y, Z), 1)
    row = lax.broadcasted_iota(jnp.int32, (Y, Z), 0)

    def pack_z(values, x, packed):
        up, down = packed
        for k, v in enumerate(ALONG_Z[0]):
            at = lane_of(k, x)
            up = jnp.where(lane == at, pltpu.roll(values(v), at + 1, 1), up)
        for k, v in enumerate(ALONG_Z[1]):
            at = lane_of(k, x)
            down = jnp.where(lane == at, pltpu.roll(values(v), at, 1), down)
        return up, down

    nothing = jnp.zeros((Y, Z), jnp.float32)

    def pack_y(field):
        for side, first in ((0, BASE + Y - 1), (1, BASE)):
            for k, v in enumerate(ALONG_Y[side]):
                ysend[field, side, k] = fields[field, SLOT[v], pl.ds(first, X, stride=Y), :]

    def sends(field):
        def copy(src, dst, steps):
            return pltpu.make_async_remote_copy(
                src_ref=src, dst_ref=dst, send_sem=send_sem.at[field], recv_sem=recv_sem.at[field],
                device_id=device(*steps), device_id_type=MESH,
            )

        buf = fields.at[field]
        last = BASE + (X - 1) * Y
        copies = [
            copy(buf.at[pl.ds(0, 5), pl.ds(last, Y), :], buf.at[pl.ds(0, 5), pl.ds(BASE - Y, Y), :], (1, 0, 0)),
            copy(buf.at[pl.ds(5, 5), pl.ds(BASE, Y), :], buf.at[pl.ds(5, 5), pl.ds(last + Y, Y), :], (-1, 0, 0)),
        ]
        for side, sz in ((0, 1), (1, -1)):
            src = zsend.at[field, side]
            for place, steps in enumerate(((0, 0, sz), (1, 0, sz), (-1, 0, sz), (0, 1, sz), (0, -1, sz))):
                copies.append(copy(src, zrecv.at[field, side, place], steps))
        for side, sy in ((0, 1), (1, -1)):
            copies.append(
                copy(ysend.at[field, side], yrecv.at[field, side, :, pl.ds(Y, X), :], (0, sy, 0))
            )
            for k, v in enumerate(ALONG_Y[side]):
                cx = VELOCITY[v][0]
                if cx:
                    at = 0 if cx > 0 else 2 * Y
                    copies.append(
                        copy(ysend.at[field, side, k], yrecv.at[field, side, k, pl.ds(at, Y), :], (cx, sy, 0))
                    )
        for c in copies:
            c.start()

    def wait_all(sem):
        rows = pops.at[pl.ds(0, 17), pl.ds(0, 2 * Y), :]
        pltpu.make_async_copy(rows, rows, sem).wait()

    def assemble_z(field):
        tiles = []
        for side in range(2):
            face, left, right, below, above = (zrecv[field, side, n] for n in range(5))
            tile = face
            for k, v in enumerate(ALONG_Z[side]):
                cx, cy, _ = VELOCITY[v]
                if cx > 0:
                    tile = jnp.where(lane == lane_of(k, -1), pltpu.roll(left, Z - X, 1), tile)
                if cx < 0:
                    tile = jnp.where(lane == lane_of(k, X), pltpu.roll(right, X, 1), tile)
                group = (lane >= 16 * k) & (lane < 16 * k + 16)
                if cy > 0:
                    moved = pltpu.roll(jnp.where(row == Y - 1, below, face), 1, 0)
                    tile = jnp.where(group, moved, tile)
                if cy < 0:
                    moved = pltpu.roll(jnp.where(row == 0, above, face), Y - 1, 0)
                    tile = jnp.where(group, moved, tile)
            tiles.append(tile)
        return tiles

    def streamed(field, x, tiles):
        result = {}
        for v in range(19):
            cx, cy, cz = VELOCITY[v]
            at = BASE + Y * (x - cx)
            if cy == 0:
                value = fields[field, SLOT[v], pl.ds(pl.multiple_of(at, Y), Y), :]
            else:
                side = 0 if cy > 0 else 1
                k = ALONG_Y[side].index(v)
                value = fields[field, SLOT[v], pl.ds(at - cy, Y), :]
                halo = yrecv[field, side, k, pl.ds(Y + x - cx, 1), :]
                value = jnp.where(row == (0 if cy > 0 else Y - 1), halo, value)
            if cz > 0:
                at = lane_of(ALONG_Z[0].index(v), x - cx)
                value = jnp.where(lane == 0, pltpu.roll(tiles[0], Z - at, 1), pltpu.roll(value, 1, 1))
            if cz < 0:
                at = lane_of(ALONG_Z[1].index(v), x - cx)
                value = jnp.where(lane == Z - 1, pltpu.roll(tiles[1], Z - 1 - at, 1), pltpu.roll(value, Z - 1, 1))
            result[v] = value
        return result

    def put(field, x, values):
        at = pl.multiple_of(BASE + Y * x, Y)
        for v in range(19):
            fields[field, SLOT[v], pl.ds(at, Y), :] = values[v]

    def plane(ref, x):
        return ref[:, pl.ds(pl.multiple_of(Y * x, Y), Y), :]

    for c in load_seed:
        c.wait()

    def pack_seed(x, packed):
        at = pl.multiple_of(BASE + Y * x, Y)
        return pack_z(lambda v: fields[seed, SLOT[v], pl.ds(at, Y), :], x, packed)

    up, down = lax.fori_loop(0, X, pack_seed, (nothing, nothing))
    zsend[seed, 0], zsend[seed, 1] = up, down
    pack_y(seed)
    pl.semaphore_wait(barrier, len(neighbours))
    sends(seed)

    for c in load_rest:
        c.wait()

    def first(x, packed):
        f = {v: pops[v, pl.ds(pl.multiple_of(Y * x, Y), Y), :] for v in range(19)}
        collided = collide(f, slip[x], perm[x], kind[x])
        put(col, x, collided)
        return pack_z(lambda v: collided[v], x, packed)

    up, down = lax.fori_loop(0, X, first, (nothing, nothing))
    zsend[col, 0], zsend[col, 1] = up, down
    pack_y(col)
    sends(col)

    wait_all(recv_sem.at[seed])
    wait_all(recv_sem.at[col])
    tiles_seed, tiles_col = assemble_z(seed), assemble_z(col)

    def second(x, packed):
        f = streamed(col, x, tiles_col)
        moved = streamed(seed, x, tiles_seed)
        g = {i: moved[OPPOSITE[i]] for i in range(19)}
        result, of_slip, of_perm = pull(f, g, slip[x], perm[x], kind[x])
        gslip[x], gperm[x] = of_slip, of_perm
        turned = {OPPOSITE[i]: result[i] for i in range(19)}
        put(grad, x, turned)
        return pack_z(lambda v: turned[v], x, packed)

    up, down = lax.fori_loop(0, X, second, (nothing, nothing))
    zsend[grad, 0], zsend[grad, 1] = up, down
    pack_y(grad)
    sends(grad)

    wait_all(recv_sem.at[grad])
    tiles_grad = assemble_z(grad)

    def third(x, carry):
        f = {v: pops[v, pl.ds(pl.multiple_of(Y * x, Y), Y), :] for v in range(19)}
        moved = streamed(grad, x, tiles_grad)
        g = {i: moved[OPPOSITE[i]] for i in range(19)}
        result, of_slip, of_perm = pull(f, g, slip[x], perm[x], kind[x])
        for v in range(19):
            out[v, x] = result[v]
        gslip[x] = gslip[x] + of_slip
        gperm[x] = gperm[x] + of_perm
        return carry

    lax.fori_loop(0, X, third, 0)
    stores = [
        pltpu.make_async_copy(src, dst, store_sem.at[n])
        for n, (src, dst) in enumerate(((out, gpop_hbm), (gslip, gslip_hbm), (gperm, gperm_hbm)))
    ]
    for c in stores:
        c.start()
    for c in stores:
        c.wait()
    for field in (seed, col, grad):
        wait_all(send_sem.at[field])


def body(populations, adjoint_seed, wall_slip, permeability, cell_kinds):
    f32 = jnp.float32
    anywhere = pl.BlockSpec(memory_space=pl.ANY)
    call = pl.pallas_call(
        kernel,
        out_shape=(
            jax.ShapeDtypeStruct((19, X, Y, Z), f32),
            jax.ShapeDtypeStruct((X, Y, Z), f32),
            jax.ShapeDtypeStruct((X, Y, Z), f32),
        ),
        in_specs=[anywhere] * 5,
        out_specs=(anywhere,) * 3,
        scratch_shapes=[
            pltpu.VMEM((19, X * Y, Z), f32),
            pltpu.VMEM((19, X, Y, Z), f32),
            pltpu.VMEM((X, Y, Z), f32),
            pltpu.VMEM((X, Y, Z), f32),
            pltpu.VMEM((X, Y, Z), jnp.int32),
            pltpu.VMEM((X, Y, Z), f32),
            pltpu.VMEM((X, Y, Z), f32),
            pltpu.VMEM((3, 19, ROWS, Z), f32),
            pltpu.VMEM((3, 2, 5, X, Z), f32),
            pltpu.VMEM((3, 2, Y, Z), f32),
            pltpu.VMEM((3, 2, 5, 3 * Y, Z), f32),
            pltpu.VMEM((3, 2, 5, Y, Z), f32),
            pltpu.SemaphoreType.DMA((23,)),
            pltpu.SemaphoreType.DMA((3,)),
            pltpu.SemaphoreType.DMA((3,)),
            pltpu.SemaphoreType.DMA((3,)),
        ],
        compiler_params=pltpu.CompilerParams(
            collective_id=0, has_side_effects=True, vmem_limit_bytes=16 * 1024 * 1024
        ),
    )
    return call(
        populations.reshape(19, X * Y, Z),
        adjoint_seed.reshape(19, X * Y, Z),
        wall_slip,
        permeability,
        cell_kinds,
    )


def solution(mesh):
    state, field = P(None, "gx", "gy", "gz"), P("gx", "gy", "gz")
    return jax.shard_map(
        body,
        mesh=mesh,
        in_specs=(state, state, field, field, field),
        out_specs=(state, field, field),
        check_vma=False,
    )
```

profile of v0, /device:TPU:32, one launch (start us, length us, event | category | flops | bytes accessed | tf_op | source)
XLA Modules:
  0.0 37.9 jit_solution(5816571354443917977)
XLA Ops:
  0.6 0.0 copy-start
  0.6 1.1 %copy-done = f32[19,8,8,128]{3,2,1,0:T(8,128)S(1)} copy-done((f32[19,8,8,128]{3,2,1,0:T(8,128)S(1)}, f32[19,8,8,128]{3,2,1,0:T(8,128)}, u32[]{:S(2)}) %copy-start) | copy-done | bytes 622616
  1.7 0.0 copy-start.1
  1.7 1.1 %copy-done.1 = f32[19,8,8,128]{3,2,1,0:T(8,128)S(1)} copy-done((f32[19,8,8,128]{3,2,1,0:T(8,128)S(1)}, f32[19,8,8,128]{3,2,1,0:T(8,128)}, u32[]{:S(2)}) %copy-start.1) | copy-done | bytes 622616
  2.8 0.0 copy-start.2
  2.8 0.8 %copy-done.2 = f32[8,8,128]{2,1,0:T(8,128)S(1)} copy-done((f32[8,8,128]{2,1,0:T(8,128)S(1)}, f32[8,8,128]{2,1,0:T(8,128)}, u32[]{:S(2)}) %copy-start.2) | copy-done | bytes 32792
  3.5 0.0 copy-start.3
  3.5 0.8 %copy-done.3 = f32[8,8,128]{2,1,0:T(8,128)S(1)} copy-done((f32[8,8,128]{2,1,0:T(8,128)S(1)}, f32[8,8,128]{2,1,0:T(8,128)}, u32[]{:S(2)}) %copy-start.3) | copy-done | bytes 32792
  4.3 0.0 copy-start.4
  4.3 0.8 %copy-done.4 = s32[8,8,128]{2,1,0:T(8,128)S(1)} copy-done((s32[8,8,128]{2,1,0:T(8,128)S(1)}, s32[8,8,128]{2,1,0:T(8,128)}, u32[]{:S(2)}) %copy-start.4) | copy-done | bytes 32792
  5.1 30.8 %shard_map.76 = (f32[19,8,8,128]{3,2,1,0:T(8,128)S(1)}, f32[8,8,128]{2,1,0:T(8,128)S(1)}, f32[8,8,128]{2,1,0:T(8,128)S(1)}) custom-call(f32[19,64,128]{2,1,0:T(8,128)S(1)} %bitcast.2, f32[19,64,128]{2,1,0:T(8,128)S(1)} %bitcast.3, f32[8,8,128]{2,1,0:T(8,128)S(1)} %copy-done.2, f32[8,8,128]{2,1,0:T(8,128)S(1)} %copy-done.3, s32[8,8,128]{2,1,0:T(8,128)S(1)} %copy-done.4), custom_call_target="tpu_custom_call" | custom-call | tf_op jit(solution)/shard_map/pallas_call | solution.py:394
  35.8 0.8 %copy.11 = f32[19,8,8,128]{3,2,1,0:T(8,128)} copy(f32[19,8,8,128]{3,2,1,0:T(8,128)S(1)} %get-tuple-element.6) | data formatting | bytes 1245184
  36.7 0.6 %copy.12 = f32[8,8,128]{2,1,0:T(8,128)} copy(f32[8,8,128]{2,1,0:T(8,128)S(1)} %get-tuple-element.7) | data formatting | bytes 65536
  37.3 0.6 %copy.13 = f32[8,8,128]{2,1,0:T(8,128)} copy(f32[8,8,128]{2,1,0:T(8,128)S(1)} %get-tuple-element.8) | data formatting | bytes 65536
Async XLA Ops:
  0.6 1.1 %copy-start = (f32[19,8,8,128]{3,2,1,0:T(8,128)S(1)}, f32[19,8,8,128]{3,2,1,0:T(8,128)}, u32[]{:S(2)}) copy-start(f32[19,8,8,128]{3,2,1,0:T(8,128)} %param.5) | copy-start | bytes 1867780
  1.7 1.1 %copy-start.1 = (f32[19,8,8,128]{3,2,1,0:T(8,128)S(1)}, f32[19,8,8,128]{3,2,1,0:T(8,128)}, u32[]{:S(2)}) copy-start(f32[19,8,8,128]{3,2,1,0:T(8,128)} %param.6) | copy-start | bytes 1867780
  2.8 0.8 %copy-start.2 = (f32[8,8,128]{2,1,0:T(8,128)S(1)}, f32[8,8,128]{2,1,0:T(8,128)}, u32[]{:S(2)}) copy-start(f32[8,8,128]{2,1,0:T(8,128)} %slip_hbm.1) | copy-start | bytes 98308
  3.5 0.8 %copy-start.3 = (f32[8,8,128]{2,1,0:T(8,128)S(1)}, f32[8,8,128]{2,1,0:T(8,128)}, u32[]{:S(2)}) copy-start(f32[8,8,128]{2,1,0:T(8,128)} %perm_hbm.1) | copy-start | bytes 98308
  4.3 0.8 %copy-start.4 = (s32[8,8,128]{2,1,0:T(8,128)S(1)}, s32[8,8,128]{2,1,0:T(8,128)}, u32[]{:S(2)}) copy-start(s32[8,8,128]{2,1,0:T(8,128)} %kind_hbm.1) | copy-start | bytes 98308
where the time goes:
time: 38.3 us; the launch traced here: 37.9 us
  Pallas kernels  30.8 us (80%)
  local copies, waits for them, and re-layouts  6.47 us (17%)
  between operations  0.65 us (2%)
    pallas_call x1, Pallas kernels, body(): call(populations.reshape(19, X * Y, Z), adjoint_seed.reshape(19, X * Y, Z...  30.8 us
    unnamed x13, local copies, waits for them, and re-layouts  6.47 us

commit v1 on v0

--- a/solution.py
+++ b/solution.py
@@ -18,8 +18,8 @@
 ALONG_Z = ((5, 11, 14, 15, 18), (6, 12, 13, 16, 17))
 W0, W1, W2 = 1.0 / 3.0, 1.0 / 18.0, 1.0 / 36.0
 X, Y, Z = 8, 8, 128
-BASE = 16
-ROWS = 96
+BASE = 8
+ROWS = 80
 
 
 def lane_of(k, x):
@@ -140,21 +140,31 @@
 
 def kernel(
     pop_hbm, seed_hbm, slip_hbm, perm_hbm, kind_hbm,
-    gpop_hbm, gslip_hbm, gperm_hbm,
-    pops, out, slip, perm, kind, gslip, gperm, fields, ysend, zsend, yrecv, zrecv,
-    load_sem, store_sem, send_sem, recv_sem,
+    out, gslip, gperm,
+    pops, slip, perm, kind, fields, ysend, zsend, xrecv, yrecv, zrecv, xyrecv, xzrecv, yzrecv,
+    load_sem, send_sem, recv_sem,
 ):
     here = tuple(lax.axis_index(a) for a in ("gx", "gy", "gz"))
     sizes = tuple(lax.axis_size(a) for a in ("gx", "gy", "gz"))
 
-    def device(*steps):
+    def device(steps):
         return tuple(
             lax.rem(h + (s + n), n) if s else h for h, s, n in zip(here, steps, sizes)
         )
 
-    neighbours = [c for c in VELOCITY if any(c)]
+    neighbours = sorted((c for c in VELOCITY if any(c)), key=lambda c: (-abs(c[0]), -sum(map(abs, c))))
     col, seed, grad = 0, 1, 2
 
+    barrier = pltpu.get_barrier_semaphore()
+    for c in neighbours:
+        pl.semaphore_signal(barrier, inc=1, device_id=device(c), device_id_type=MESH)
+
+    load_rest = [
+        pltpu.make_async_copy(src, dst, load_sem.at[19 + n])
+        for n, (src, dst) in enumerate(
+            ((pop_hbm, pops), (slip_hbm, slip), (perm_hbm, perm), (kind_hbm, kind))
+        )
+    ]
     load_seed = [
         pltpu.make_async_copy(
             seed_hbm.at[i],
@@ -163,20 +173,8 @@
         )
         for i in range(19)
     ]
-    for c in load_seed:
+    for c in load_rest + load_seed:
         c.start()
-    load_rest = [
-        pltpu.make_async_copy(src, dst, load_sem.at[19 + n])
-        for n, (src, dst) in enumerate(
-            ((pop_hbm, pops), (slip_hbm, slip), (perm_hbm, perm), (kind_hbm, kind))
-        )
-    ]
-    for c in load_rest:
-        c.start()
-
-    barrier = pltpu.get_barrier_semaphore()
-    for c in neighbours:
-        pl.semaphore_signal(barrier, inc=1, device_id=device(*c), device_id_type=MESH)
 
     lane = lax.broadcasted_iota(jnp.int32, (Y, Z), 1)
     row = lax.broadcasted_iota(jnp.int32, (Y, Z), 0)
@@ -198,74 +196,91 @@
             for k, v in enumerate(ALONG_Y[side]):
                 ysend[field, side, k] = fields[field, SLOT[v], pl.ds(first, X, stride=Y), :]
 
-    def sends(field):
+    def copies_of(which, turn):
         def copy(src, dst, steps):
+            n = 2 * turn + (0 if steps[0] else 1)
             return pltpu.make_async_remote_copy(
-                src_ref=src, dst_ref=dst, send_sem=send_sem.at[field], recv_sem=recv_sem.at[field],
-                device_id=device(*steps), device_id_type=MESH,
+                src_ref=src, dst_ref=dst, send_sem=send_sem.at[n], recv_sem=recv_sem.at[n],
+                device_id=device(steps), device_id_type=MESH,
             )
 
-        buf = fields.at[field]
+        far, near = [], []
         last = BASE + (X - 1) * Y
-        copies = [
-            copy(buf.at[pl.ds(0, 5), pl.ds(last, Y), :], buf.at[pl.ds(0, 5), pl.ds(BASE - Y, Y), :], (1, 0, 0)),
-            copy(buf.at[pl.ds(5, 5), pl.ds(BASE, Y), :], buf.at[pl.ds(5, 5), pl.ds(last + Y, Y), :], (-1, 0, 0)),
-        ]
-        for side, sz in ((0, 1), (1, -1)):
-            src = zsend.at[field, side]
-            for place, steps in enumerate(((0, 0, sz), (1, 0, sz), (-1, 0, sz), (0, 1, sz), (0, -1, sz))):
-                copies.append(copy(src, zrecv.at[field, side, place], steps))
-        for side, sy in ((0, 1), (1, -1)):
-            copies.append(
-                copy(ysend.at[field, side], yrecv.at[field, side, :, pl.ds(Y, X), :], (0, sy, 0))
-            )
+        for side, (at, cx) in enumerate(((last, 1), (BASE, -1))):
+            far.append(copy(
+                fields.at[which, pl.ds(5 * side, 5), pl.ds(at, Y), :],
+                xrecv.at[which, side, :, pl.ds(Y, Y), :], (cx, 0, 0),
+            ))
+        for side, cy in ((0, 1), (1, -1)):
             for k, v in enumerate(ALONG_Y[side]):
                 cx = VELOCITY[v][0]
                 if cx:
-                    at = 0 if cx > 0 else 2 * Y
-                    copies.append(
-                        copy(ysend.at[field, side, k], yrecv.at[field, side, k, pl.ds(at, Y), :], (cx, sy, 0))
-                    )
-        for c in copies:
-            c.start()
-
-    def wait_all(sem):
-        rows = pops.at[pl.ds(0, 17), pl.ds(0, 2 * Y), :]
-        pltpu.make_async_copy(rows, rows, sem).wait()
-
-    def assemble_z(field):
+                    x = X - 1 if cx > 0 else 0
+                    far.append(copy(
+                        ysend.at[which, side, k, pl.ds(x, 1), :],
+                        xyrecv.at[which, side, 0 if cx > 0 else 1], (cx, cy, 0),
+                    ))
+            near.append(copy(ysend.at[which, side], yrecv.at[which, side], (0, cy, 0)))
+        for side, cz in ((0, 1), (1, -1)):
+            src = zsend.at[which, side]
+            for n, c in enumerate((1, -1)):
+                far.append(copy(src, xzrecv.at[which, side, n], (c, 0, cz)))
+                near.append(copy(src, yzrecv.at[which, side, n], (0, c, cz)))
+            near.append(copy(src, zrecv.at[which, side], (0, 0, cz)))
+        return far, near
+
+    def wait_all(sem, rows):
+        depth = 58 if rows % 58 == 0 else 64
+        some = pops.at[pl.ds(0, rows // depth), pl.ds(0, depth), :]
+        pltpu.make_async_copy(some, some, sem).wait()
+
+    def near_tiles(field):
         tiles = []
         for side in range(2):
-            face, left, right, below, above = (zrecv[field, side, n] for n in range(5))
+            face = zrecv[field, side]
             tile = face
             for k, v in enumerate(ALONG_Z[side]):
-                cx, cy, _ = VELOCITY[v]
-                if cx > 0:
-                    tile = jnp.where(lane == lane_of(k, -1), pltpu.roll(left, Z - X, 1), tile)
-                if cx < 0:
-                    tile = jnp.where(lane == lane_of(k, X), pltpu.roll(right, X, 1), tile)
+                cy = VELOCITY[v][1]
                 group = (lane >= 16 * k) & (lane < 16 * k + 16)
                 if cy > 0:
-                    moved = pltpu.roll(jnp.where(row == Y - 1, below, face), 1, 0)
+                    moved = pltpu.roll(jnp.where(row == Y - 1, yzrecv[field, side, 0], face), 1, 0)
                     tile = jnp.where(group, moved, tile)
                 if cy < 0:
-                    moved = pltpu.roll(jnp.where(row == 0, above, face), Y - 1, 0)
+                    moved = pltpu.roll(jnp.where(row == 0, yzrecv[field, side, 1], face), Y - 1, 0)
                     tile = jnp.where(group, moved, tile)
             tiles.append(tile)
         return tiles
+
+    def all_tiles(field, tiles):
+        result = []
+        for side, tile in enumerate(tiles):
+            for k, v in enumerate(ALONG_Z[side]):
+                cx = VELOCITY[v][0]
+                if cx > 0:
+                    tile = jnp.where(lane == lane_of(k, -1), pltpu.roll(xzrecv[field, side, 0], Z - X, 1), tile)
+                if cx < 0:
+                    tile = jnp.where(lane == lane_of(k, X), pltpu.roll(xzrecv[field, side, 1], X, 1), tile)
+            result.append(tile)
+        return result
 
     def streamed(field, x, tiles):
         result = {}
         for v in range(19):
             cx, cy, cz = VELOCITY[v]
-            at = BASE + Y * (x - cx)
-            if cy == 0:
-                value = fields[field, SLOT[v], pl.ds(pl.multiple_of(at, Y), Y), :]
+            outside = isinstance(x, int) and not 0 <= x - cx < X
+            if outside:
+                end = 0 if cx > 0 else 1
+                value = xrecv[field, end, SLOT[v] - 5 * end, pl.ds(Y - cy, Y), :]
+            elif cy:
+                value = fields[field, SLOT[v], pl.ds(BASE + Y * (x - cx) - cy, Y), :]
             else:
+                value = fields[field, SLOT[v], pl.ds(pl.multiple_of(BASE + Y * (x - cx), Y), Y), :]
+            if cy:
                 side = 0 if cy > 0 else 1
-                k = ALONG_Y[side].index(v)
-                value = fields[field, SLOT[v], pl.ds(at - cy, Y), :]
-                halo = yrecv[field, side, k, pl.ds(Y + x - cx, 1), :]
+                if outside:
+                    halo = xyrecv[field, side, end]
+                else:
+                    halo = yrecv[field, side, ALONG_Y[side].index(v), pl.ds(x - cx, 1), :]
                 value = jnp.where(row == (0 if cy > 0 else Y - 1), halo, value)
             if cz > 0:
                 at = lane_of(ALONG_Z[0].index(v), x - cx)
@@ -281,8 +296,9 @@
         for v in range(19):
             fields[field, SLOT[v], pl.ds(at, Y), :] = values[v]
 
-    def plane(ref, x):
-        return ref[:, pl.ds(pl.multiple_of(Y * x, Y), Y), :]
+    def start(copies):
+        for c in copies:
+            c.start()
 
     for c in load_seed:
         c.wait()
@@ -294,8 +310,6 @@
     up, down = lax.fori_loop(0, X, pack_seed, (nothing, nothing))
     zsend[seed, 0], zsend[seed, 1] = up, down
     pack_y(seed)
-    pl.semaphore_wait(barrier, len(neighbours))
-    sends(seed)
 
     for c in load_rest:
         c.wait()
@@ -309,13 +323,13 @@
     up, down = lax.fori_loop(0, X, first, (nothing, nothing))
     zsend[col, 0], zsend[col, 1] = up, down
     pack_y(col)
-    sends(col)
-
-    wait_all(recv_sem.at[seed])
-    wait_all(recv_sem.at[col])
-    tiles_seed, tiles_col = assemble_z(seed), assemble_z(col)
-
-    def second(x, packed):
+
+    both = pl.ds(0, 2)
+    pl.semaphore_wait(barrier, len(neighbours))
+    far, near = copies_of(both, 0)
+    start(far + near)
+
+    def second(x, packed, tiles_col, tiles_seed):
         f = streamed(col, x, tiles_col)
         moved = streamed(seed, x, tiles_seed)
         g = {i: moved[OPPOSITE[i]] for i in range(19)}
@@ -325,79 +339,104 @@
         put(grad, x, turned)
         return pack_z(lambda v: turned[v], x, packed)
 
-    up, down = lax.fori_loop(0, X, second, (nothing, nothing))
-    zsend[grad, 0], zsend[grad, 1] = up, down
+    FAR, NEAR = 2 * 5 * Y + 4 + 4 * Y, 2 * 5 * Y + 6 * Y
+    wait_all(recv_sem.at[1], 2 * NEAR)
+    tiles_col, tiles_seed = near_tiles(col), near_tiles(seed)
+    packed = lax.fori_loop(1, X - 1, lambda x, p: second(x, p, tiles_col, tiles_seed), (nothing, nothing))
+    wait_all(recv_sem.at[0], 2 * FAR)
+    tiles_col, tiles_seed = all_tiles(col, tiles_col), all_tiles(seed, tiles_seed)
+    for x in (0, X - 1):
+        packed = second(x, packed, tiles_col, tiles_seed)
+    zsend[grad, 0], zsend[grad, 1] = packed
     pack_y(grad)
-    sends(grad)
-
-    wait_all(recv_sem.at[grad])
-    tiles_grad = assemble_z(grad)
-
-    def third(x, carry):
+    far, near = copies_of(grad, 1)
+    start(far + near)
+
+    def third(x, tiles):
         f = {v: pops[v, pl.ds(pl.multiple_of(Y * x, Y), Y), :] for v in range(19)}
-        moved = streamed(grad, x, tiles_grad)
+        moved = streamed(grad, x, tiles)
         g = {i: moved[OPPOSITE[i]] for i in range(19)}
         result, of_slip, of_perm = pull(f, g, slip[x], perm[x], kind[x])
         for v in range(19):
             out[v, x] = result[v]
         gslip[x] = gslip[x] + of_slip
         gperm[x] = gperm[x] + of_perm
+
+    def inner(x, carry):
+        third(x, tiles)
         return carry
 
-    lax.fori_loop(0, X, third, 0)
-    stores = [
-        pltpu.make_async_copy(src, dst, store_sem.at[n])
-        for n, (src, dst) in enumerate(((out, gpop_hbm), (gslip, gslip_hbm), (gperm, gperm_hbm)))
+    wait_all(recv_sem.at[3], NEAR)
+    tiles = near_tiles(grad)
+    lax.fori_loop(1, X - 1, inner, 0)
+    for n, rows in ((0, 2 * FAR), (1, 2 * NEAR), (3, NEAR)):
+        wait_all(send_sem.at[n], rows)
+    wait_all(recv_sem.at[2], FAR)
+    tiles = all_tiles(grad, tiles)
+    for x in (0, X - 1):
+        third(x, tiles)
+    wait_all(send_sem.at[2], FAR)
+
+
+def store(out, gslip, gperm, out_hbm, gslip_hbm, gperm_hbm, sem):
+    copies = [
+        pltpu.make_async_copy(src, dst, sem.at[n])
+        for n, (src, dst) in enumerate(((out, out_hbm), (gslip, gslip_hbm), (gperm, gperm_hbm)))
     ]
-    for c in stores:
+    for c in copies:
         c.start()
-    for c in stores:
+    for c in copies:
         c.wait()
-    for field in (seed, col, grad):
-        wait_all(send_sem.at[field])
 
 
 def body(populations, adjoint_seed, wall_slip, permeability, cell_kinds):
     f32 = jnp.float32
-    anywhere = pl.BlockSpec(memory_space=pl.ANY)
+    hbm = pl.BlockSpec(memory_space=pltpu.HBM)
+    resident = pl.BlockSpec(memory_space=pltpu.VMEM)
+    shapes = ((19, X, Y, Z), (X, Y, Z), (X, Y, Z))
     call = pl.pallas_call(
         kernel,
-        out_shape=(
-            jax.ShapeDtypeStruct((19, X, Y, Z), f32),
-            jax.ShapeDtypeStruct((X, Y, Z), f32),
-            jax.ShapeDtypeStruct((X, Y, Z), f32),
-        ),
-        in_specs=[anywhere] * 5,
-        out_specs=(anywhere,) * 3,
+        out_shape=tuple(pltpu.VMEM(shape, f32) for shape in shapes),
+        in_specs=[hbm] * 5,
+        out_specs=(resident,) * 3,
         scratch_shapes=[
             pltpu.VMEM((19, X * Y, Z), f32),
-            pltpu.VMEM((19, X, Y, Z), f32),
             pltpu.VMEM((X, Y, Z), f32),
             pltpu.VMEM((X, Y, Z), f32),
             pltpu.VMEM((X, Y, Z), jnp.int32),
-            pltpu.VMEM((X, Y, Z), f32),
-            pltpu.VMEM((X, Y, Z), f32),
             pltpu.VMEM((3, 19, ROWS, Z), f32),
             pltpu.VMEM((3, 2, 5, X, Z), f32),
             pltpu.VMEM((3, 2, Y, Z), f32),
             pltpu.VMEM((3, 2, 5, 3 * Y, Z), f32),
-            pltpu.VMEM((3, 2, 5, Y, Z), f32),
+            pltpu.VMEM((3, 2, 5, X, Z), f32),
+            pltpu.VMEM((3, 2, Y, Z), f32),
+            pltpu.VMEM((3, 2, 2, 1, Z), f32),
+            pltpu.VMEM((3, 2, 2, Y, Z), f32),
+            pltpu.VMEM((3, 2, 2, Y, Z), f32),
             pltpu.SemaphoreType.DMA((23,)),
-            pltpu.SemaphoreType.DMA((3,)),
-            pltpu.SemaphoreType.DMA((3,)),
-            pltpu.SemaphoreType.DMA((3,)),
+            pltpu.SemaphoreType.DMA((4,)),
+            pltpu.SemaphoreType.DMA((4,)),
         ],
         compiler_params=pltpu.CompilerParams(
             collective_id=0, has_side_effects=True, vmem_limit_bytes=16 * 1024 * 1024
         ),
     )
-    return call(
+    operands = (
         populations.reshape(19, X * Y, Z),
         adjoint_seed.reshape(19, X * Y, Z),
         wall_slip,
         permeability,
         cell_kinds,
     )
+    results = call(*(pltpu.with_memory_space_constraint(a, pltpu.HBM) for a in operands))
+    return pl.pallas_call(
+        store,
+        out_shape=tuple(jax.ShapeDtypeStruct(shape, f32) for shape in shapes),
+        in_specs=[resident] * 3,
+        out_specs=(hbm,) * 3,
+        scratch_shapes=[pltpu.SemaphoreType.DMA((3,))],
+        compiler_params=pltpu.CompilerParams(vmem_limit_bytes=1024 * 1024),
+    )(*(pltpu.with_memory_space_constraint(a, pltpu.VMEM) for a in results))
 
 
 def solution(mesh):

time: 38.3 us -> 26.8 us (0.70)
  local copies, waits for them, and re-layouts: 6.47 us -> 0 us
  Pallas kernels: 30.8 us -> 25.7 us
    unnamed x13 -> x0, local copies, waits for them, and re-layouts: 6.47 us -> none
    pallas_call x1 -> x2, Pallas kernels: 30.8 us -> 25.7 us  [the longest x1 24.8 us: body(): call(*(pltpu.with_memory_space_constraint(a, pltpu.HBM) for a in operands))]
where the time goes in v1:
time: 26.8 us; the launch traced here: 26.3 us
  Pallas kernels  25.7 us (96%)
  between operations  0.64 us (2%)
    pallas_call x1, Pallas kernels, body(): call(*(pltpu.with_memory_space_constraint(a, pltpu.HBM) for a in operands))  24.8 us
    pallas_call x1, Pallas kernels, body(): pl.pallas_call(store, out_shape=tuple((jax.ShapeDtypeStruct(shape, f32) f...  0.86 us

profile of v1, /device:TPU:32, one launch (start us, length us, event | category | flops | bytes accessed | tf_op | source)
XLA Modules:
  0.0 26.3 jit_solution(11926406116677600917)
XLA Ops:
  0.6 24.8 %shard_map.76 = (f32[19,8,8,128]{3,2,1,0:T(8,128)S(1)}, f32[8,8,128]{2,1,0:T(8,128)S(1)}, f32[8,8,128]{2,1,0:T(8,128)S(1)}) custom-call(f32[19,64,128]{2,1,0:T(8,128)} %bitcast.2, f32[19,64,128]{2,1,0:T(8,128)} %bitcast.3, f32[8,8,128]{2,1,0:T(8,128)} %slip_hbm.1, f32[8,8,128]{2,1,0:T(8,128)} %perm_hbm.1, s32[8,8,128]{2,1,0:T(8,128)} %kind_hbm.1), custom_call_target="tpu_custom_call" | custom-call | tf_op jit(solution)/shard_map/pallas_call | solution.py:431
  25.5 0.9 %shard_map.77 = (f32[19,8,8,128]{3,2,1,0:T(8,128)}, f32[8,8,128]{2,1,0:T(8,128)}, f32[8,8,128]{2,1,0:T(8,128)}) custom-call(f32[19,8,8,128]{3,2,1,0:T(8,128)S(1)} %get-tuple-element.6.out, f32[8,8,128]{2,1,0:T(8,128)S(1)} %get-tuple-element.7.gslip, f32[8,8,128]{2,1,0:T(8,128)S(1)} %get-tuple-element.8.gperm), custom_call_target="tpu_custom_call" | custom-call | tf_op jit(solution)/shard_map/pallas_call | solution.py:432

commit v2 on v1

--- a/solution.py
+++ b/solution.py
@@ -22,8 +22,8 @@
 ROWS = 80
 
 
-def lane_of(k, x):
-    return 16 * k + x + 1
+def lane_of(group, x):
+    return 10 * group + x + 1
 
 
 def pairs_of(f):
@@ -152,7 +152,7 @@
             lax.rem(h + (s + n), n) if s else h for h, s, n in zip(here, steps, sizes)
         )
 
-    neighbours = sorted((c for c in VELOCITY if any(c)), key=lambda c: (-abs(c[0]), -sum(map(abs, c))))
+    neighbours = sorted((c for c in VELOCITY if any(c)), key=lambda c: (-abs(c[0]), -abs(c[1]), -sum(map(abs, c))))
     col, seed, grad = 0, 1, 2
 
     barrier = pltpu.get_barrier_semaphore()
@@ -179,13 +179,13 @@
     lane = lax.broadcasted_iota(jnp.int32, (Y, Z), 1)
     row = lax.broadcasted_iota(jnp.int32, (Y, Z), 0)
 
-    def pack_z(values, x, packed):
+    def pack_z(values, x, packed, member):
         up, down = packed
         for k, v in enumerate(ALONG_Z[0]):
-            at = lane_of(k, x)
+            at = lane_of(5 * member + k, x)
             up = jnp.where(lane == at, pltpu.roll(values(v), at + 1, 1), up)
         for k, v in enumerate(ALONG_Z[1]):
-            at = lane_of(k, x)
+            at = lane_of(5 * member + k, x)
             down = jnp.where(lane == at, pltpu.roll(values(v), at, 1), down)
         return up, down
 
@@ -196,74 +196,74 @@
             for k, v in enumerate(ALONG_Y[side]):
                 ysend[field, side, k] = fields[field, SLOT[v], pl.ds(first, X, stride=Y), :]
 
-    def copies_of(which, turn):
-        def copy(src, dst, steps):
-            n = 2 * turn + (0 if steps[0] else 1)
-            return pltpu.make_async_remote_copy(
-                src_ref=src, dst_ref=dst, send_sem=send_sem.at[n], recv_sem=recv_sem.at[n],
-                device_id=device(steps), device_id_type=MESH,
-            )
-
-        far, near = [], []
-        last = BASE + (X - 1) * Y
-        for side, (at, cx) in enumerate(((last, 1), (BASE, -1))):
-            far.append(copy(
-                fields.at[which, pl.ds(5 * side, 5), pl.ds(at, Y), :],
-                xrecv.at[which, side, :, pl.ds(Y, Y), :], (cx, 0, 0),
-            ))
+    def copy(src, dst, steps, n):
+        return pltpu.make_async_remote_copy(
+            src_ref=src, dst_ref=dst, send_sem=send_sem.at[n], recv_sem=recv_sem.at[n],
+            device_id=device(steps), device_id_type=MESH,
+        )
+
+    def diagonals(which):
         for side, cy in ((0, 1), (1, -1)):
             for k, v in enumerate(ALONG_Y[side]):
                 cx = VELOCITY[v][0]
                 if cx:
-                    x = X - 1 if cx > 0 else 0
-                    far.append(copy(
-                        ysend.at[which, side, k, pl.ds(x, 1), :],
-                        xyrecv.at[which, side, 0 if cx > 0 else 1], (cx, cy, 0),
-                    ))
-            near.append(copy(ysend.at[which, side], yrecv.at[which, side], (0, cy, 0)))
+                    src = ysend.at[which, side, k, pl.ds(X - 1 if cx > 0 else 0, 1), :]
+                    yield src, (which, side, 0 if cx > 0 else 1), cx, cy
+
+    def copies_of(which, turn):
+        xs, xz, near = [], [], []
+        FAR, NEAR = 2 * turn, 2 * turn + 1
+        last = BASE + (X - 1) * Y
+        for side, (at, cx) in enumerate(((last, 1), (BASE, -1))):
+            xs.append(copy(
+                fields.at[which, pl.ds(5 * side, 5), pl.ds(at, Y), :],
+                xrecv.at[which, side, :, pl.ds(Y, Y), :], (cx, 0, 0), FAR,
+            ))
+        for side, cy in ((0, 1), (1, -1)):
+            near.append(copy(ysend.at[which, side], yrecv.at[which, side], (0, cy, 0), NEAR))
         for side, cz in ((0, 1), (1, -1)):
-            src = zsend.at[which, side]
+            tile = zsend.at[turn, side]
+            near.append(copy(tile, zrecv.at[turn, side], (0, 0, cz), NEAR))
             for n, c in enumerate((1, -1)):
-                far.append(copy(src, xzrecv.at[which, side, n], (c, 0, cz)))
-                near.append(copy(src, yzrecv.at[which, side, n], (0, c, cz)))
-            near.append(copy(src, zrecv.at[which, side], (0, 0, cz)))
-        return far, near
+                xz.append(copy(tile, xzrecv.at[turn, side, n], (c, 0, cz), FAR))
+                end = zsend.at[turn, side, pl.ds(Y - 1 if c > 0 else 0, 1), :]
+                near.append(copy(end, yzrecv.at[turn, side, n], (0, c, cz), NEAR))
+        return xs, xz, near
 
     def wait_all(sem, rows):
-        depth = 58 if rows % 58 == 0 else 64
+        depth = next(d for d in (58, 50, 60, 8) if rows % d == 0)
         some = pops.at[pl.ds(0, rows // depth), pl.ds(0, depth), :]
         pltpu.make_async_copy(some, some, sem).wait()
 
-    def near_tiles(field):
+    def lanes(turn, side, wanted, xs):
+        mask = None
+        for group in range(10 if turn == 0 else 5):
+            if wanted(VELOCITY[ALONG_Z[side][group % 5]]):
+                a, b = lane_of(group, xs[0]), lane_of(group, xs[1])
+                here = (lane >= a) & (lane <= b)
+                mask = here if mask is None else mask | here
+        return mask
+
+    def near_tiles(turn):
         tiles = []
         for side in range(2):
-            face = zrecv[field, side]
-            tile = face
-            for k, v in enumerate(ALONG_Z[side]):
-                cy = VELOCITY[v][1]
-                group = (lane >= 16 * k) & (lane < 16 * k + 16)
-                if cy > 0:
-                    moved = pltpu.roll(jnp.where(row == Y - 1, yzrecv[field, side, 0], face), 1, 0)
-                    tile = jnp.where(group, moved, tile)
-                if cy < 0:
-                    moved = pltpu.roll(jnp.where(row == 0, yzrecv[field, side, 1], face), Y - 1, 0)
-                    tile = jnp.where(group, moved, tile)
-            tiles.append(tile)
+            face = zrecv[turn, side]
+            up = jnp.where(row == 0, yzrecv[turn, side, 0], pltpu.roll(face, 1, 0))
+            down = jnp.where(row == Y - 1, yzrecv[turn, side, 1], pltpu.roll(face, Y - 1, 0))
+            tile = jnp.where(lanes(turn, side, lambda c: c[1] > 0, (-1, X)), up, face)
+            tiles.append(jnp.where(lanes(turn, side, lambda c: c[1] < 0, (-1, X)), down, tile))
         return tiles
 
-    def all_tiles(field, tiles):
+    def all_tiles(turn, tiles):
         result = []
         for side, tile in enumerate(tiles):
-            for k, v in enumerate(ALONG_Z[side]):
-                cx = VELOCITY[v][0]
-                if cx > 0:
-                    tile = jnp.where(lane == lane_of(k, -1), pltpu.roll(xzrecv[field, side, 0], Z - X, 1), tile)
-                if cx < 0:
-                    tile = jnp.where(lane == lane_of(k, X), pltpu.roll(xzrecv[field, side, 1], X, 1), tile)
-            result.append(tile)
+            left = pltpu.roll(xzrecv[turn, side, 0], Z - X, 1)
+            right = pltpu.roll(xzrecv[turn, side, 1], X, 1)
+            tile = jnp.where(lanes(turn, side, lambda c: c[0] > 0, (-1, -1)), left, tile)
+            result.append(jnp.where(lanes(turn, side, lambda c: c[0] < 0, (X, X)), right, tile))
         return result
 
-    def streamed(field, x, tiles):
+    def streamed(field, x, tiles, member):
         result = {}
         for v in range(19):
             cx, cy, cz = VELOCITY[v]
@@ -283,10 +283,10 @@
                     halo = yrecv[field, side, ALONG_Y[side].index(v), pl.ds(x - cx, 1), :]
                 value = jnp.where(row == (0 if cy > 0 else Y - 1), halo, value)
             if cz > 0:
-                at = lane_of(ALONG_Z[0].index(v), x - cx)
+                at = lane_of(5 * member + ALONG_Z[0].index(v), x - cx)
                 value = jnp.where(lane == 0, pltpu.roll(tiles[0], Z - at, 1), pltpu.roll(value, 1, 1))
             if cz < 0:
-                at = lane_of(ALONG_Z[1].index(v), x - cx)
+                at = lane_of(5 * member + ALONG_Z[1].index(v), x - cx)
                 value = jnp.where(lane == Z - 1, pltpu.roll(tiles[1], Z - 1 - at, 1), pltpu.roll(value, Z - 1, 1))
             result[v] = value
         return result
@@ -305,10 +305,9 @@
 
     def pack_seed(x, packed):
         at = pl.multiple_of(BASE + Y * x, Y)
-        return pack_z(lambda v: fields[seed, SLOT[v], pl.ds(at, Y), :], x, packed)
-
-    up, down = lax.fori_loop(0, X, pack_seed, (nothing, nothing))
-    zsend[seed, 0], zsend[seed, 1] = up, down
+        return pack_z(lambda v: fields[seed, SLOT[v], pl.ds(at, Y), :], x, packed, 1)
+
+    packed = lax.fori_loop(0, X, pack_seed, (nothing, nothing))
     pack_y(seed)
 
     for c in load_rest:
@@ -318,43 +317,41 @@
         f = {v: pops[v, pl.ds(pl.multiple_of(Y * x, Y), Y), :] for v in range(19)}
         collided = collide(f, slip[x], perm[x], kind[x])
         put(col, x, collided)
-        return pack_z(lambda v: collided[v], x, packed)
-
-    up, down = lax.fori_loop(0, X, first, (nothing, nothing))
-    zsend[col, 0], zsend[col, 1] = up, down
+        return pack_z(lambda v: collided[v], x, packed, 0)
+
+    zsend[0, 0], zsend[0, 1] = lax.fori_loop(0, X, first, packed)
     pack_y(col)
 
     both = pl.ds(0, 2)
     pl.semaphore_wait(barrier, len(neighbours))
-    far, near = copies_of(both, 0)
-    start(far + near)
-
-    def second(x, packed, tiles_col, tiles_seed):
-        f = streamed(col, x, tiles_col)
-        moved = streamed(seed, x, tiles_seed)
+    xs, xz, near = copies_of(both, 0)
+    start([copy(src, xyrecv.at[at], (cx, cy, 0), 0) for src, at, cx, cy in diagonals(both)] + xs + xz + near)
+
+    def second(x, packed, tiles):
+        f = streamed(col, x, tiles, 0)
+        moved = streamed(seed, x, tiles, 1)
         g = {i: moved[OPPOSITE[i]] for i in range(19)}
         result, of_slip, of_perm = pull(f, g, slip[x], perm[x], kind[x])
         gslip[x], gperm[x] = of_slip, of_perm
         turned = {OPPOSITE[i]: result[i] for i in range(19)}
         put(grad, x, turned)
-        return pack_z(lambda v: turned[v], x, packed)
-
-    FAR, NEAR = 2 * 5 * Y + 4 + 4 * Y, 2 * 5 * Y + 6 * Y
-    wait_all(recv_sem.at[1], 2 * NEAR)
-    tiles_col, tiles_seed = near_tiles(col), near_tiles(seed)
-    packed = lax.fori_loop(1, X - 1, lambda x, p: second(x, p, tiles_col, tiles_seed), (nothing, nothing))
-    wait_all(recv_sem.at[0], 2 * FAR)
-    tiles_col, tiles_seed = all_tiles(col, tiles_col), all_tiles(seed, tiles_seed)
+        return pack_z(lambda v: turned[v], x, packed, 0)
+
+    wait_all(recv_sem.at[1], 180)
+    tiles = near_tiles(0)
+    packed = lax.fori_loop(1, X - 1, lambda x, p: second(x, p, tiles), (nothing, nothing))
+    wait_all(recv_sem.at[0], 200)
+    tiles = all_tiles(0, tiles)
     for x in (0, X - 1):
-        packed = second(x, packed, tiles_col, tiles_seed)
-    zsend[grad, 0], zsend[grad, 1] = packed
+        packed = second(x, packed, tiles)
+    zsend[1, 0], zsend[1, 1] = packed
     pack_y(grad)
-    far, near = copies_of(grad, 1)
-    start(far + near)
+    xs, xz, near = copies_of(grad, 1)
+    start([copy(src, xyrecv.at[at], (cx, cy, 0), 2) for src, at, cx, cy in diagonals(grad)] + xs + xz + near)
 
     def third(x, tiles):
         f = {v: pops[v, pl.ds(pl.multiple_of(Y * x, Y), Y), :] for v in range(19)}
-        moved = streamed(grad, x, tiles)
+        moved = streamed(grad, x, tiles, 0)
         g = {i: moved[OPPOSITE[i]] for i in range(19)}
         result, of_slip, of_perm = pull(f, g, slip[x], perm[x], kind[x])
         for v in range(19):
@@ -366,16 +363,16 @@
         third(x, tiles)
         return carry
 
-    wait_all(recv_sem.at[3], NEAR)
-    tiles = near_tiles(grad)
+    wait_all(recv_sem.at[3], 100)
+    tiles = near_tiles(1)
     lax.fori_loop(1, X - 1, inner, 0)
-    for n, rows in ((0, 2 * FAR), (1, 2 * NEAR), (3, NEAR)):
+    for n, rows in ((0, 200), (1, 180), (3, 100)):
         wait_all(send_sem.at[n], rows)
-    wait_all(recv_sem.at[2], FAR)
-    tiles = all_tiles(grad, tiles)
+    wait_all(recv_sem.at[2], 116)
+    tiles = all_tiles(1, tiles)
     for x in (0, X - 1):
         third(x, tiles)
-    wait_all(send_sem.at[2], FAR)
+    wait_all(send_sem.at[2], 116)
 
 
 def store(out, gslip, gperm, out_hbm, gslip_hbm, gperm_hbm, sem):
@@ -406,13 +403,13 @@
             pltpu.VMEM((X, Y, Z), jnp.int32),
             pltpu.VMEM((3, 19, ROWS, Z), f32),
             pltpu.VMEM((3, 2, 5, X, Z), f32),
-            pltpu.VMEM((3, 2, Y, Z), f32),
+            pltpu.VMEM((2, 2, Y, Z), f32),
             pltpu.VMEM((3, 2, 5, 3 * Y, Z), f32),
             pltpu.VMEM((3, 2, 5, X, Z), f32),
-            pltpu.VMEM((3, 2, Y, Z), f32),
+            pltpu.VMEM((2, 2, Y, Z), f32),
             pltpu.VMEM((3, 2, 2, 1, Z), f32),
-            pltpu.VMEM((3, 2, 2, Y, Z), f32),
-            pltpu.VMEM((3, 2, 2, Y, Z), f32),
+            pltpu.VMEM((2, 2, 2, Y, Z), f32),
+            pltpu.VMEM((2, 2, 2, 1, Z), f32),
             pltpu.SemaphoreType.DMA((23,)),
             pltpu.SemaphoreType.DMA((4,)),
             pltpu.SemaphoreType.DMA((4,)),

time: 26.8 us -> 25.4 us (0.948); the launches traced: 26.3 us -> 25.2 us
  Pallas kernels: 25.7 us -> 24.6 us
    pallas_call x1, Pallas kernels: 24.8 us -> 23.7 us  [body(): call(*(pltpu.with_memory_space_constraint(a, pltpu.HBM) for a in operands))]
where the time goes in v2:
time: 25.4 us; the launch traced here: 25.2 us
  Pallas kernels  24.6 us (97%)
  between operations  0.64 us (3%)
    pallas_call x1, Pallas kernels, body(): call(*(pltpu.with_memory_space_constraint(a, pltpu.HBM) for a in operands))  23.7 us
    pallas_call x1, Pallas kernels, body(): pl.pallas_call(store, out_shape=tuple((jax.ShapeDtypeStruct(shape, f32) f...  0.86 us

profile of v2, /device:TPU:32, one launch (start us, length us, event | category | flops | bytes accessed | tf_op | source)
XLA Modules:
  0.0 25.2 jit_solution(6270079189689819900)
XLA Ops:
  0.6 23.7 %shard_map.76 = (f32[19,8,8,128]{3,2,1,0:T(8,128)S(1)}, f32[8,8,128]{2,1,0:T(8,128)S(1)}, f32[8,8,128]{2,1,0:T(8,128)S(1)}) custom-call(f32[19,64,128]{2,1,0:T(8,128)} %bitcast.2, f32[19,64,128]{2,1,0:T(8,128)} %bitcast.3, f32[8,8,128]{2,1,0:T(8,128)} %slip_hbm.1, f32[8,8,128]{2,1,0:T(8,128)} %perm_hbm.1, s32[8,8,128]{2,1,0:T(8,128)} %kind_hbm.1), custom_call_target="tpu_custom_call" | custom-call | tf_op jit(solution)/shard_map/pallas_call | solution.py:428
  24.4 0.9 %shard_map.77 = (f32[19,8,8,128]{3,2,1,0:T(8,128)}, f32[8,8,128]{2,1,0:T(8,128)}, f32[8,8,128]{2,1,0:T(8,128)}) custom-call(f32[19,8,8,128]{3,2,1,0:T(8,128)S(1)} %get-tuple-element.6.out, f32[8,8,128]{2,1,0:T(8,128)S(1)} %get-tuple-element.7.gslip, f32[8,8,128]{2,1,0:T(8,128)S(1)} %get-tuple-element.8.gperm), custom_call_target="tpu_custom_call" | custom-call | tf_op jit(solution)/shard_map/pallas_call | solution.py:429

commit v3 on v2

--- a/solution.py
+++ b/solution.py
@@ -147,10 +147,11 @@
     here = tuple(lax.axis_index(a) for a in ("gx", "gy", "gz"))
     sizes = tuple(lax.axis_size(a) for a in ("gx", "gy", "gz"))
 
+    above = tuple(lax.rem(h + 1, n) for h, n in zip(here, sizes))
+    below = tuple(lax.rem(h + n - 1, n) for h, n in zip(here, sizes))
+
     def device(steps):
-        return tuple(
-            lax.rem(h + (s + n), n) if s else h for h, s, n in zip(here, steps, sizes)
-        )
+        return tuple((h, up, down)[s] for s, h, up, down in zip(steps, here, above, below))
 
     neighbours = sorted((c for c in VELOCITY if any(c)), key=lambda c: (-abs(c[0]), -abs(c[1]), -sum(map(abs, c))))
     col, seed, grad = 0, 1, 2
@@ -204,10 +205,11 @@
 
     def diagonals(which):
         for side, cy in ((0, 1), (1, -1)):
-            for k, v in enumerate(ALONG_Y[side]):
+            for v in ALONG_Y[side]:
                 cx = VELOCITY[v][0]
                 if cx:
-                    src = ysend.at[which, side, k, pl.ds(X - 1 if cx > 0 else 0, 1), :]
+                    at = BASE + (X - 1) * Y * (cx > 0) + (Y - 1) * (cy > 0)
+                    src = fields.at[which, SLOT[v], pl.ds(at, 1), :]
                     yield src, (which, side, 0 if cx > 0 else 1), cx, cy
 
     def copies_of(which, turn):
@@ -254,27 +256,19 @@
             tiles.append(jnp.where(lanes(turn, side, lambda c: c[1] < 0, (-1, X)), down, tile))
         return tiles
 
-    def all_tiles(turn, tiles):
-        result = []
-        for side, tile in enumerate(tiles):
-            left = pltpu.roll(xzrecv[turn, side, 0], Z - X, 1)
-            right = pltpu.roll(xzrecv[turn, side, 1], X, 1)
-            tile = jnp.where(lanes(turn, side, lambda c: c[0] > 0, (-1, -1)), left, tile)
-            result.append(jnp.where(lanes(turn, side, lambda c: c[0] < 0, (X, X)), right, tile))
-        return result
-
-    def streamed(field, x, tiles, member):
+    def streamed(field, x, tiles, member, ends):
+        turn = 1 if field == grad else 0
         result = {}
         for v in range(19):
             cx, cy, cz = VELOCITY[v]
-            outside = isinstance(x, int) and not 0 <= x - cx < X
+            outside = not 0 <= x - cx < X
+            if outside != ends:
+                continue
+            end = 0 if cx > 0 else 1
             if outside:
-                end = 0 if cx > 0 else 1
                 value = xrecv[field, end, SLOT[v] - 5 * end, pl.ds(Y - cy, Y), :]
-            elif cy:
+            else:
                 value = fields[field, SLOT[v], pl.ds(BASE + Y * (x - cx) - cy, Y), :]
-            else:
-                value = fields[field, SLOT[v], pl.ds(pl.multiple_of(BASE + Y * (x - cx), Y), Y), :]
             if cy:
                 side = 0 if cy > 0 else 1
                 if outside:
@@ -282,17 +276,20 @@
                 else:
                     halo = yrecv[field, side, ALONG_Y[side].index(v), pl.ds(x - cx, 1), :]
                 value = jnp.where(row == (0 if cy > 0 else Y - 1), halo, value)
-            if cz > 0:
-                at = lane_of(5 * member + ALONG_Z[0].index(v), x - cx)
-                value = jnp.where(lane == 0, pltpu.roll(tiles[0], Z - at, 1), pltpu.roll(value, 1, 1))
-            if cz < 0:
-                at = lane_of(5 * member + ALONG_Z[1].index(v), x - cx)
-                value = jnp.where(lane == Z - 1, pltpu.roll(tiles[1], Z - 1 - at, 1), pltpu.roll(value, Z - 1, 1))
+            if cz:
+                side = 0 if cz > 0 else 1
+                group = 5 * member + ALONG_Z[side].index(v)
+                tile = xzrecv[turn, side, end] if outside else tiles[side]
+                at = lane_of(group, (x - cx) % X)
+                edge, shift = (0, 1) if cz > 0 else (Z - 1, Z - 1)
+                value = jnp.where(
+                    lane == edge, pltpu.roll(tile, (edge - at) % Z, 1), pltpu.roll(value, shift, 1)
+                )
             result[v] = value
         return result
 
     def put(field, x, values):
-        at = pl.multiple_of(BASE + Y * x, Y)
+        at = BASE + Y * x
         for v in range(19):
             fields[field, SLOT[v], pl.ds(at, Y), :] = values[v]
 
@@ -303,55 +300,63 @@
     for c in load_seed:
         c.wait()
 
-    def pack_seed(x, packed):
-        at = pl.multiple_of(BASE + Y * x, Y)
-        return pack_z(lambda v: fields[seed, SLOT[v], pl.ds(at, Y), :], x, packed, 1)
-
-    packed = lax.fori_loop(0, X, pack_seed, (nothing, nothing))
+    packed = (nothing, nothing)
+    for x in range(X):
+        packed = pack_z(lambda v: fields[seed, SLOT[v], pl.ds(BASE + Y * x, Y), :], x, packed, 1)
     pack_y(seed)
 
     for c in load_rest:
         c.wait()
 
-    def first(x, packed):
-        f = {v: pops[v, pl.ds(pl.multiple_of(Y * x, Y), Y), :] for v in range(19)}
+    for x in range(X):
+        f = {v: pops[v, pl.ds(Y * x, Y), :] for v in range(19)}
         collided = collide(f, slip[x], perm[x], kind[x])
         put(col, x, collided)
-        return pack_z(lambda v: collided[v], x, packed, 0)
-
-    zsend[0, 0], zsend[0, 1] = lax.fori_loop(0, X, first, packed)
+        packed = pack_z(lambda v: collided[v], x, packed, 0)
+    zsend[0, 0], zsend[0, 1] = packed
     pack_y(col)
 
     both = pl.ds(0, 2)
     pl.semaphore_wait(barrier, len(neighbours))
     xs, xz, near = copies_of(both, 0)
-    start([copy(src, xyrecv.at[at], (cx, cy, 0), 0) for src, at, cx, cy in diagonals(both)] + xs + xz + near)
-
-    def second(x, packed, tiles):
-        f = streamed(col, x, tiles, 0)
-        moved = streamed(seed, x, tiles, 1)
+    nz, ny = near[2:], near[:2]
+    start([copy(src, xyrecv.at[at], (cx, cy, 0), 0) for src, at, cx, cy in diagonals(both)] + nz + xz + xs + ny)
+
+    def inside(x, tiles):
+        return streamed(col, x, tiles, 0, False), streamed(seed, x, tiles, 1, False)
+
+    def second(x, tiles, known):
+        f = known[0] | streamed(col, x, tiles, 0, True)
+        moved = known[1] | streamed(seed, x, tiles, 1, True)
         g = {i: moved[OPPOSITE[i]] for i in range(19)}
         result, of_slip, of_perm = pull(f, g, slip[x], perm[x], kind[x])
         gslip[x], gperm[x] = of_slip, of_perm
         turned = {OPPOSITE[i]: result[i] for i in range(19)}
         put(grad, x, turned)
-        return pack_z(lambda v: turned[v], x, packed, 0)
+        return turned
 
     wait_all(recv_sem.at[1], 180)
     tiles = near_tiles(0)
-    packed = lax.fori_loop(1, X - 1, lambda x, p: second(x, p, tiles), (nothing, nothing))
+    packed = (nothing, nothing)
+    for x in range(1, X - 1):
+        turned = second(x, tiles, inside(x, tiles))
+        packed = pack_z(lambda v: turned[v], x, packed, 0)
+    known = {x: inside(x, tiles) for x in (0, X - 1)}
     wait_all(recv_sem.at[0], 200)
-    tiles = all_tiles(0, tiles)
-    for x in (0, X - 1):
-        packed = second(x, packed, tiles)
+    ends = {x: second(x, tiles, known[x]) for x in (0, X - 1)}
+    xs, xz, near = copies_of(grad, 1)
+    nz, ny = near[2:], near[:2]
+    start([copy(src, xyrecv.at[at], (cx, cy, 0), 2) for src, at, cx, cy in diagonals(grad)] + xs)
+    for x, turned in ends.items():
+        packed = pack_z(lambda v: turned[v], x, packed, 0)
     zsend[1, 0], zsend[1, 1] = packed
+    start(nz + xz)
     pack_y(grad)
-    xs, xz, near = copies_of(grad, 1)
-    start([copy(src, xyrecv.at[at], (cx, cy, 0), 2) for src, at, cx, cy in diagonals(grad)] + xs + xz + near)
-
-    def third(x, tiles):
-        f = {v: pops[v, pl.ds(pl.multiple_of(Y * x, Y), Y), :] for v in range(19)}
-        moved = streamed(grad, x, tiles, 0)
+    start(ny)
+
+    def third(x, tiles, known):
+        f = {v: pops[v, pl.ds(Y * x, Y), :] for v in range(19)}
+        moved = known | streamed(grad, x, tiles, 0, True)
         g = {i: moved[OPPOSITE[i]] for i in range(19)}
         result, of_slip, of_perm = pull(f, g, slip[x], perm[x], kind[x])
         for v in range(19):
@@ -359,19 +364,16 @@
         gslip[x] = gslip[x] + of_slip
         gperm[x] = gperm[x] + of_perm
 
-    def inner(x, carry):
-        third(x, tiles)
-        return carry
-
     wait_all(recv_sem.at[3], 100)
     tiles = near_tiles(1)
-    lax.fori_loop(1, X - 1, inner, 0)
+    for x in range(1, X - 1):
+        third(x, tiles, streamed(grad, x, tiles, 0, False))
+    known = {x: streamed(grad, x, tiles, 0, False) for x in (0, X - 1)}
     for n, rows in ((0, 200), (1, 180), (3, 100)):
         wait_all(send_sem.at[n], rows)
     wait_all(recv_sem.at[2], 116)
-    tiles = all_tiles(1, tiles)
     for x in (0, X - 1):
-        third(x, tiles)
+        third(x, tiles, known[x])
     wait_all(send_sem.at[2], 116)
 
 

time: 25.4 us -> 25 us (0.984)
  Pallas kernels: 24.6 us -> 24.3 us
    pallas_call x1, Pallas kernels: 23.7 us -> 23.4 us  [body(): call(*(pltpu.with_memory_space_constraint(a, pltpu.HBM) for a in operands))]
where the time goes in v3:
time: 25 us; the launch traced here: 24.9 us
  Pallas kernels  24.3 us (97%)
  between operations  0.64 us (3%)
    pallas_call x1, Pallas kernels, body(): call(*(pltpu.with_memory_space_constraint(a, pltpu.HBM) for a in operands))  23.4 us
    pallas_call x1, Pallas kernels, body(): pl.pallas_call(store, out_shape=tuple((jax.ShapeDtypeStruct(shape, f32) f...  0.86 us

profile of v3, /device:TPU:32, one launch (start us, length us, event | category | flops | bytes accessed | tf_op | source)
XLA Modules:
  0.0 24.9 jit_solution(15811519446760293452)
XLA Ops:
  0.6 23.4 %shard_map.76 = (f32[19,8,8,128]{3,2,1,0:T(8,128)S(1)}, f32[8,8,128]{2,1,0:T(8,128)S(1)}, f32[8,8,128]{2,1,0:T(8,128)S(1)}) custom-call(f32[19,64,128]{2,1,0:T(8,128)} %bitcast.2, f32[19,64,128]{2,1,0:T(8,128)} %bitcast.3, f32[8,8,128]{2,1,0:T(8,128)} %slip_hbm.1, f32[8,8,128]{2,1,0:T(8,128)} %perm_hbm.1, s32[8,8,128]{2,1,0:T(8,128)} %kind_hbm.1), custom_call_target="tpu_custom_call" | custom-call | tf_op jit(solution)/shard_map/pallas_call | solution.py:430
  24.1 0.9 %shard_map.77 = (f32[19,8,8,128]{3,2,1,0:T(8,128)}, f32[8,8,128]{2,1,0:T(8,128)}, f32[8,8,128]{2,1,0:T(8,128)}) custom-call(f32[19,8,8,128]{3,2,1,0:T(8,128)S(1)} %get-tuple-element.6.out, f32[8,8,128]{2,1,0:T(8,128)S(1)} %get-tuple-element.7.gslip, f32[8,8,128]{2,1,0:T(8,128)S(1)} %get-tuple-element.8.gperm), custom_call_target="tpu_custom_call" | custom-call | tf_op jit(solution)/shard_map/pallas_call | solution.py:431

commit v4 on v3

--- a/solution.py
+++ b/solution.py
@@ -141,7 +141,7 @@
 def kernel(
     pop_hbm, seed_hbm, slip_hbm, perm_hbm, kind_hbm,
     out, gslip, gperm,
-    pops, slip, perm, kind, fields, ysend, zsend, xrecv, yrecv, zrecv, xyrecv, xzrecv, yzrecv,
+    pops, slip, perm, kind, fields, ysend, zsend, xrecv, yrecv, zrecv, hop, xyrecv, xzrecv, yzrecv,
     load_sem, send_sem, recv_sem,
 ):
     here = tuple(lax.axis_index(a) for a in ("gx", "gy", "gz"))
@@ -156,9 +156,18 @@
     neighbours = sorted((c for c in VELOCITY if any(c)), key=lambda c: (-abs(c[0]), -abs(c[1]), -sum(map(abs, c))))
     col, seed, grad = 0, 1, 2
 
+    detours = (here[0] == 0) & (here[1] == 0)
+    passes_on = (here[0] == sizes[0] - 1) & (here[1] == 0)
+
     barrier = pltpu.get_barrier_semaphore()
     for c in neighbours:
-        pl.semaphore_signal(barrier, inc=1, device_id=device(c), device_id_type=MESH)
+        def greet(c=c):
+            pl.semaphore_signal(barrier, inc=1, device_id=device(c), device_id_type=MESH)
+
+        if c[0] == 1 and c[1]:
+            pl.when(jnp.logical_not((here[0] == sizes[0] - 1) & (device(c)[1] == 0)))(greet)
+        else:
+            greet()
 
     load_rest = [
         pltpu.make_async_copy(src, dst, load_sem.at[19 + n])
@@ -197,9 +206,10 @@
             for k, v in enumerate(ALONG_Y[side]):
                 ysend[field, side, k] = fields[field, SLOT[v], pl.ds(first, X, stride=Y), :]
 
-    def copy(src, dst, steps, n):
+    def copy(src, dst, steps, n, arrives=None):
+        arrives = n if arrives is None else arrives
         return pltpu.make_async_remote_copy(
-            src_ref=src, dst_ref=dst, send_sem=send_sem.at[n], recv_sem=recv_sem.at[n],
+            src_ref=src, dst_ref=dst, send_sem=send_sem.at[n], recv_sem=recv_sem.at[arrives],
             device_id=device(steps), device_id_type=MESH,
         )
 
@@ -233,7 +243,7 @@
         return xs, xz, near
 
     def wait_all(sem, rows):
-        depth = next(d for d in (58, 50, 60, 8) if rows % d == 0)
+        depth = next(d for d in (58, 50, 60, 4) if rows % d == 0)
         some = pops.at[pl.ds(0, rows // depth), pl.ds(0, depth), :]
         pltpu.make_async_copy(some, some, sem).wait()
 
@@ -317,10 +327,22 @@
     pack_y(col)
 
     both = pl.ds(0, 2)
-    pl.semaphore_wait(barrier, len(neighbours))
+    pl.semaphore_wait(barrier, len(neighbours) - 2 * detours.astype(jnp.int32))
     xs, xz, near = copies_of(both, 0)
     nz, ny = near[2:], near[:2]
-    start([copy(src, xyrecv.at[at], (cx, cy, 0), 0) for src, at, cx, cy in diagonals(both)] + nz + xz + xs + ny)
+
+    @pl.when(detours)
+    def _():
+        start([
+            copy(src, xyrecv.at[at], (cx, cy, 0), 0) if cx > 0 else copy(src, hop.at[at[:2]], (cx, 0, 0), 0, 4)
+            for src, at, cx, cy in diagonals(both)
+        ])
+
+    @pl.when(jnp.logical_not(detours))
+    def _():
+        start([copy(src, xyrecv.at[at], (cx, cy, 0), 0) for src, at, cx, cy in diagonals(both)])
+
+    start(nz + xz + xs + ny)
 
     def inside(x, tiles):
         return streamed(col, x, tiles, 0, False), streamed(seed, x, tiles, 1, False)
@@ -342,6 +364,15 @@
         turned = second(x, tiles, inside(x, tiles))
         packed = pack_z(lambda v: turned[v], x, packed, 0)
     known = {x: inside(x, tiles) for x in (0, X - 1)}
+
+    @pl.when(passes_on)
+    def _():
+        wait_all(recv_sem.at[4], 4)
+        start([
+            copy(hop.at[both, side], xyrecv.at[both, side, 1], (0, cy, 0), 4, 0)
+            for side, cy in ((0, 1), (1, -1))
+        ])
+
     wait_all(recv_sem.at[0], 200)
     ends = {x: second(x, tiles, known[x]) for x in (0, X - 1)}
     xs, xz, near = copies_of(grad, 1)
@@ -371,6 +402,11 @@
     known = {x: streamed(grad, x, tiles, 0, False) for x in (0, X - 1)}
     for n, rows in ((0, 200), (1, 180), (3, 100)):
         wait_all(send_sem.at[n], rows)
+
+    @pl.when(passes_on)
+    def _():
+        wait_all(send_sem.at[4], 4)
+
     wait_all(recv_sem.at[2], 116)
     for x in (0, X - 1):
         third(x, tiles, known[x])
@@ -409,12 +445,13 @@
             pltpu.VMEM((3, 2, 5, 3 * Y, Z), f32),
             pltpu.VMEM((3, 2, 5, X, Z), f32),
             pltpu.VMEM((2, 2, Y, Z), f32),
+            pltpu.VMEM((2, 2, 1, Z), f32),
             pltpu.VMEM((3, 2, 2, 1, Z), f32),
             pltpu.VMEM((2, 2, 2, Y, Z), f32),
             pltpu.VMEM((2, 2, 2, 1, Z), f32),
             pltpu.SemaphoreType.DMA((23,)),
-            pltpu.SemaphoreType.DMA((4,)),
-            pltpu.SemaphoreType.DMA((4,)),
+            pltpu.SemaphoreType.DMA((5,)),
+            pltpu.SemaphoreType.DMA((5,)),
         ],
         compiler_params=pltpu.CompilerParams(
             collective_id=0, has_side_effects=True, vmem_limit_bytes=16 * 1024 * 1024

time: 25 us -> 24.1 us (0.964)
  Pallas kernels: 24.3 us -> 23.3 us
    pallas_call x1, Pallas kernels: 23.4 us -> 22.4 us  [body(): call(*(pltpu.with_memory_space_constraint(a, pltpu.HBM) for a in operands))]
where the time goes in v4:
time: 24.1 us; the launch traced here: 23.9 us
  Pallas kernels  23.3 us (97%)
  between operations  0.64 us (3%)
    pallas_call x1, Pallas kernels, body(): call(*(pltpu.with_memory_space_constraint(a, pltpu.HBM) for a in operands))  22.4 us
    pallas_call x1, Pallas kernels, body(): pl.pallas_call(store, out_shape=tuple((jax.ShapeDtypeStruct(shape, f32) f...  0.86 us

profile of v4, /device:TPU:32, one launch (start us, length us, event | category | flops | bytes accessed | tf_op | source)
XLA Modules:
  0.0 23.9 jit_solution(12144783739445250880)
XLA Ops:
  0.6 22.4 %shard_map.76 = (f32[19,8,8,128]{3,2,1,0:T(8,128)S(1)}, f32[8,8,128]{2,1,0:T(8,128)S(1)}, f32[8,8,128]{2,1,0:T(8,128)S(1)}) custom-call(f32[19,64,128]{2,1,0:T(8,128)} %bitcast.2, f32[19,64,128]{2,1,0:T(8,128)} %bitcast.3, f32[8,8,128]{2,1,0:T(8,128)} %slip_hbm.1, f32[8,8,128]{2,1,0:T(8,128)} %perm_hbm.1, s32[8,8,128]{2,1,0:T(8,128)} %kind_hbm.1), custom_call_target="tpu_custom_call" | custom-call | tf_op jit(solution)/shard_map/pallas_call | solution.py:467
  23.1 0.9 %shard_map.77 = (f32[19,8,8,128]{3,2,1,0:T(8,128)}, f32[8,8,128]{2,1,0:T(8,128)}, f32[8,8,128]{2,1,0:T(8,128)}) custom-call(f32[19,8,8,128]{3,2,1,0:T(8,128)S(1)} %get-tuple-element.6.out, f32[8,8,128]{2,1,0:T(8,128)S(1)} %get-tuple-element.7.gslip, f32[8,8,128]{2,1,0:T(8,128)S(1)} %get-tuple-element.8.gperm), custom_call_target="tpu_custom_call" | custom-call | tf_op jit(solution)/shard_map/pallas_call | solution.py:468

commit v5 on v4

--- a/solution.py
+++ b/solution.py
@@ -1,3 +1,5 @@
+import functools
+
 import jax
 import jax.numpy as jnp
 from jax import lax
@@ -149,25 +151,41 @@
 
     above = tuple(lax.rem(h + 1, n) for h, n in zip(here, sizes))
     below = tuple(lax.rem(h + n - 1, n) for h, n in zip(here, sizes))
-
-    def device(steps):
-        return tuple((h, up, down)[s] for s, h, up, down in zip(steps, here, above, below))
-
-    neighbours = sorted((c for c in VELOCITY if any(c)), key=lambda c: (-abs(c[0]), -abs(c[1]), -sum(map(abs, c))))
     col, seed, grad = 0, 1, 2
+
+    odd = lax.rem(here[0], 2)
+    ends = (1 - odd, odd)
+    across = tuple(jnp.where(end == 0, above[0], below[0]) for end in ends)
+    FARTHER, CLOSER = 0, 1
+
+    def device(place, cy, cz):
+        gy, gz = ((h, up, down)[c] for c, h, up, down in zip((cy, cz), here[1:], above[1:], below[1:]))
+        return (here[0] if place is None else across[place], gy, gz)
 
     detours = (here[0] == 0) & (here[1] == 0)
     passes_on = (here[0] == sizes[0] - 1) & (here[1] == 0)
 
     barrier = pltpu.get_barrier_semaphore()
-    for c in neighbours:
-        def greet(c=c):
-            pl.semaphore_signal(barrier, inc=1, device_id=device(c), device_id_type=MESH)
-
-        if c[0] == 1 and c[1]:
-            pl.when(jnp.logical_not((here[0] == sizes[0] - 1) & (device(c)[1] == 0)))(greet)
-        else:
-            greet()
+
+    def greet(target):
+        pl.semaphore_signal(barrier, inc=1, device_id=target, device_id_type=MESH)
+
+    SIDES = ((1, 0), (-1, 0)), ((0, 1), (0, -1))
+    for place in (FARTHER, CLOSER):
+        for cy, cz in SIDES[0]:
+            if place == FARTHER:
+                target = device(place, cy, cz)
+                spared = (here[0] == sizes[0] - 1) & (target[1] == 0)
+                pl.when(jnp.logical_not(spared))(functools.partial(greet, target))
+            else:
+                greet(device(place, cy, cz))
+        greet(device(place, 0, 0))
+        for cy, cz in SIDES[1]:
+            greet(device(place, cy, cz))
+    for cy in (1, -1, 0):
+        for cz in (1, -1, 0):
+            if cy or cz:
+                greet(device(None, cy, cz))
 
     load_rest = [
         pltpu.make_async_copy(src, dst, load_sem.at[19 + n])
@@ -206,41 +224,46 @@
             for k, v in enumerate(ALONG_Y[side]):
                 ysend[field, side, k] = fields[field, SLOT[v], pl.ds(first, X, stride=Y), :]
 
-    def copy(src, dst, steps, n, arrives=None):
+    def copy(src, dst, target, n, arrives=None):
         arrives = n if arrives is None else arrives
         return pltpu.make_async_remote_copy(
             src_ref=src, dst_ref=dst, send_sem=send_sem.at[n], recv_sem=recv_sem.at[arrives],
-            device_id=device(steps), device_id_type=MESH,
+            device_id=target, device_id_type=MESH,
         )
 
-    def diagonals(which):
+    def xy_rows(which, place, n, way=None):
+        end = ends[place]
         for side, cy in ((0, 1), (1, -1)):
-            for v in ALONG_Y[side]:
-                cx = VELOCITY[v][0]
-                if cx:
-                    at = BASE + (X - 1) * Y * (cx > 0) + (Y - 1) * (cy > 0)
-                    src = fields.at[which, SLOT[v], pl.ds(at, 1), :]
-                    yield src, (which, side, 0 if cx > 0 else 1), cx, cy
-
-    def copies_of(which, turn):
-        xs, xz, near = [], [], []
-        FAR, NEAR = 2 * turn, 2 * turn + 1
-        last = BASE + (X - 1) * Y
-        for side, (at, cx) in enumerate(((last, 1), (BASE, -1))):
-            xs.append(copy(
-                fields.at[which, pl.ds(5 * side, 5), pl.ds(at, Y), :],
-                xrecv.at[which, side, :, pl.ds(Y, Y), :], (cx, 0, 0), FAR,
-            ))
+            slot = 1 + 6 * end if cy > 0 else 2 + 4 * end
+            at = BASE + (X - 1) * Y * (1 - end) + (Y - 1) * (cy > 0)
+            src = fields.at[which, slot, pl.ds(at, 1), :]
+            if way is None:
+                yield copy(src, xyrecv.at[which, side, end], device(place, cy, 0), n)
+            else:
+                yield copy(src, way.at[which, side], device(place, 0, 0), n, 4)
+
+    def x_face(which, place, n):
+        end = ends[place]
+        at = pl.multiple_of(BASE + (X - 1) * Y * (1 - end), Y)
+        yield copy(
+            fields.at[which, pl.ds(5 * end, 5), pl.ds(at, Y), :],
+            xrecv.at[which, end, :, pl.ds(Y, Y), :], device(place, 0, 0), n,
+        )
+
+    def xz_tiles(turn, place, n):
+        for side, cz in ((0, 1), (1, -1)):
+            yield copy(zsend.at[turn, side], xzrecv.at[turn, side, ends[place]], device(place, 0, cz), n)
+
+    def y_faces(which, n):
         for side, cy in ((0, 1), (1, -1)):
-            near.append(copy(ysend.at[which, side], yrecv.at[which, side], (0, cy, 0), NEAR))
+            yield copy(ysend.at[which, side], yrecv.at[which, side], device(None, cy, 0), n)
+
+    def z_faces(turn, n):
         for side, cz in ((0, 1), (1, -1)):
-            tile = zsend.at[turn, side]
-            near.append(copy(tile, zrecv.at[turn, side], (0, 0, cz), NEAR))
-            for n, c in enumerate((1, -1)):
-                xz.append(copy(tile, xzrecv.at[turn, side, n], (c, 0, cz), FAR))
-                end = zsend.at[turn, side, pl.ds(Y - 1 if c > 0 else 0, 1), :]
-                near.append(copy(end, yzrecv.at[turn, side, n], (0, c, cz), NEAR))
-        return xs, xz, near
+            yield copy(zsend.at[turn, side], zrecv.at[turn, side], device(None, 0, cz), n)
+            for k, cy in enumerate((1, -1)):
+                row_of = zsend.at[turn, side, pl.ds(Y - 1 if cy > 0 else 0, 1), :]
+                yield copy(row_of, yzrecv.at[turn, side, k], device(None, cy, cz), n)
 
     def wait_all(sem, rows):
         depth = next(d for d in (58, 50, 60, 4) if rows % d == 0)
@@ -266,13 +289,13 @@
             tiles.append(jnp.where(lanes(turn, side, lambda c: c[1] < 0, (-1, X)), down, tile))
         return tiles
 
-    def streamed(field, x, tiles, member, ends):
+    def streamed(field, x, tiles, member, outer):
         turn = 1 if field == grad else 0
         result = {}
         for v in range(19):
             cx, cy, cz = VELOCITY[v]
             outside = not 0 <= x - cx < X
-            if outside != ends:
+            if outside != outer:
                 continue
             end = 0 if cx > 0 else 1
             if outside:
@@ -327,22 +350,16 @@
     pack_y(col)
 
     both = pl.ds(0, 2)
-    pl.semaphore_wait(barrier, len(neighbours) - 2 * detours.astype(jnp.int32))
-    xs, xz, near = copies_of(both, 0)
-    nz, ny = near[2:], near[:2]
-
-    @pl.when(detours)
-    def _():
-        start([
-            copy(src, xyrecv.at[at], (cx, cy, 0), 0) if cx > 0 else copy(src, hop.at[at[:2]], (cx, 0, 0), 0, 4)
-            for src, at, cx, cy in diagonals(both)
-        ])
-
-    @pl.when(jnp.logical_not(detours))
-    def _():
-        start([copy(src, xyrecv.at[at], (cx, cy, 0), 0) for src, at, cx, cy in diagonals(both)])
-
-    start(nz + xz + xs + ny)
+    pl.semaphore_wait(barrier, 18 - 2 * detours.astype(jnp.int32))
+    pl.when(detours)(lambda: start(xy_rows(both, FARTHER, 0, hop)))
+    pl.when(jnp.logical_not(detours))(lambda: start(xy_rows(both, FARTHER, 0)))
+    start(z_faces(0, 1))
+    start(x_face(both, FARTHER, 0))
+    start(xz_tiles(0, FARTHER, 0))
+    start(xy_rows(both, CLOSER, 0))
+    start(xz_tiles(0, CLOSER, 0))
+    start(x_face(both, CLOSER, 0))
+    start(y_faces(both, 1))
 
     def inside(x, tiles):
         return streamed(col, x, tiles, 0, False), streamed(seed, x, tiles, 1, False)
@@ -369,21 +386,24 @@
     def _():
         wait_all(recv_sem.at[4], 4)
         start([
-            copy(hop.at[both, side], xyrecv.at[both, side, 1], (0, cy, 0), 4, 0)
+            copy(hop.at[both, side], xyrecv.at[both, side, 1], device(None, cy, 0), 4, 0)
             for side, cy in ((0, 1), (1, -1))
         ])
 
     wait_all(recv_sem.at[0], 200)
-    ends = {x: second(x, tiles, known[x]) for x in (0, X - 1)}
-    xs, xz, near = copies_of(grad, 1)
-    nz, ny = near[2:], near[:2]
-    start([copy(src, xyrecv.at[at], (cx, cy, 0), 2) for src, at, cx, cy in diagonals(grad)] + xs)
-    for x, turned in ends.items():
+    outer = {x: second(x, tiles, known[x]) for x in (0, X - 1)}
+    start(xy_rows(grad, FARTHER, 2))
+    start(x_face(grad, FARTHER, 2))
+    start(xy_rows(grad, CLOSER, 2))
+    start(x_face(grad, CLOSER, 2))
+    for x, turned in outer.items():
         packed = pack_z(lambda v: turned[v], x, packed, 0)
     zsend[1, 0], zsend[1, 1] = packed
-    start(nz + xz)
+    start(z_faces(1, 3))
+    start(xz_tiles(1, FARTHER, 2))
+    start(xz_tiles(1, CLOSER, 2))
     pack_y(grad)
-    start(ny)
+    start(y_faces(grad, 3))
 
     def third(x, tiles, known):
         f = {v: pops[v, pl.ds(Y * x, Y), :] for v in range(19)}

time: 24.1 us -> 23.9 us (level)
  no operation moved by 1% of the time
where the time goes in v5:
time: 23.9 us; the launch traced here: 23.8 us
  Pallas kernels  23.2 us (97%)
  between operations  0.64 us (3%)
    pallas_call x1, Pallas kernels, body(): call(*(pltpu.with_memory_space_constraint(a, pltpu.HBM) for a in operands))  22.3 us
    pallas_call x1, Pallas kernels, body(): pl.pallas_call(store, out_shape=tuple((jax.ShapeDtypeStruct(shape, f32) f...  0.86 us

profile of v5, /device:TPU:32, one launch (start us, length us, event | category | flops | bytes accessed | tf_op | source)
XLA Modules:
  0.0 23.8 jit_solution(8829781947654168195)
XLA Ops:
  0.6 22.3 %shard_map.76 = (f32[19,8,8,128]{3,2,1,0:T(8,128)S(1)}, f32[8,8,128]{2,1,0:T(8,128)S(1)}, f32[8,8,128]{2,1,0:T(8,128)S(1)}) custom-call(f32[19,64,128]{2,1,0:T(8,128)} %bitcast.2, f32[19,64,128]{2,1,0:T(8,128)} %bitcast.3, f32[8,8,128]{2,1,0:T(8,128)} %slip_hbm.1, f32[8,8,128]{2,1,0:T(8,128)} %perm_hbm.1, s32[8,8,128]{2,1,0:T(8,128)} %kind_hbm.1), custom_call_target="tpu_custom_call" | custom-call | tf_op jit(solution)/shard_map/pallas_call | solution.py:487
  23.0 0.9 %shard_map.77 = (f32[19,8,8,128]{3,2,1,0:T(8,128)}, f32[8,8,128]{2,1,0:T(8,128)}, f32[8,8,128]{2,1,0:T(8,128)}) custom-call(f32[19,8,8,128]{3,2,1,0:T(8,128)S(1)} %get-tuple-element.6.out, f32[8,8,128]{2,1,0:T(8,128)S(1)} %get-tuple-element.7.gslip, f32[8,8,128]{2,1,0:T(8,128)S(1)} %get-tuple-element.8.gperm), custom_call_target="tpu_custom_call" | custom-call | tf_op jit(solution)/shard_map/pallas_call | solution.py:488

commit v6 on v5

--- a/solution.py
+++ b/solution.py
@@ -162,8 +162,11 @@
         gy, gz = ((h, up, down)[c] for c, h, up, down in zip((cy, cz), here[1:], above[1:], below[1:]))
         return (here[0] if place is None else across[place], gy, gz)
 
-    detours = (here[0] == 0) & (here[1] == 0)
-    passes_on = (here[0] == sizes[0] - 1) & (here[1] == 0)
+    phase, low = lax.rem(here[0], 4), here[1] == 0
+    last = here[0] == sizes[0] - 1
+    by_x, by_y = low & (here[0] == 0), low & (phase == 1)
+    detours = by_x | by_y
+    passes_on = low & last
 
     barrier = pltpu.get_barrier_semaphore()
 
@@ -175,20 +178,20 @@
         for cy, cz in SIDES[0]:
             if place == FARTHER:
                 target = device(place, cy, cz)
-                spared = (here[0] == sizes[0] - 1) & (target[1] == 0)
+                spared = (last | (phase == 2)) & (target[1] == 0)
                 pl.when(jnp.logical_not(spared))(functools.partial(greet, target))
             else:
                 greet(device(place, cy, cz))
-        greet(device(place, 0, 0))
         for cy, cz in SIDES[1]:
             greet(device(place, cy, cz))
+        greet(device(place, 0, 0))
     for cy in (1, -1, 0):
         for cz in (1, -1, 0):
             if cy or cz:
                 greet(device(None, cy, cz))
 
     load_rest = [
-        pltpu.make_async_copy(src, dst, load_sem.at[19 + n])
+        pltpu.make_async_copy(src, dst, load_sem.at[1 + n])
         for n, (src, dst) in enumerate(
             ((pop_hbm, pops), (slip_hbm, slip), (perm_hbm, perm), (kind_hbm, kind))
         )
@@ -197,7 +200,7 @@
         pltpu.make_async_copy(
             seed_hbm.at[i],
             fields.at[seed, SLOT[OPPOSITE[i]], pl.ds(BASE, X * Y), :],
-            load_sem.at[i],
+            load_sem.at[0],
         )
         for i in range(19)
     ]
@@ -240,7 +243,8 @@
             if way is None:
                 yield copy(src, xyrecv.at[which, side, end], device(place, cy, 0), n)
             else:
-                yield copy(src, way.at[which, side], device(place, 0, 0), n, 4)
+                target = device(place, 0, 0) if way == 0 else device(None, cy, 0)
+                yield copy(src, hop.at[which, side], target, n, 4)
 
     def x_face(which, place, n):
         end = ends[place]
@@ -266,7 +270,7 @@
                 yield copy(row_of, yzrecv.at[turn, side, k], device(None, cy, cz), n)
 
     def wait_all(sem, rows):
-        depth = next(d for d in (58, 50, 60, 4) if rows % d == 0)
+        depth = next(d for d in (58, 50, 60, 4, 2) if rows % d == 0)
         some = pops.at[pl.ds(0, rows // depth), pl.ds(0, depth), :]
         pltpu.make_async_copy(some, some, sem).wait()
 
@@ -330,8 +334,7 @@
         for c in copies:
             c.start()
 
-    for c in load_seed:
-        c.wait()
+    pltpu.make_async_copy(pops, pops, load_sem.at[0]).wait()
 
     packed = (nothing, nothing)
     for x in range(X):
@@ -351,15 +354,22 @@
 
     both = pl.ds(0, 2)
     pl.semaphore_wait(barrier, 18 - 2 * detours.astype(jnp.int32))
-    pl.when(detours)(lambda: start(xy_rows(both, FARTHER, 0, hop)))
+    pl.when(by_x)(lambda: start(xy_rows(both, FARTHER, 0, 0)))
+    pl.when(by_y)(lambda: start(xy_rows(both, FARTHER, 0, 1)))
     pl.when(jnp.logical_not(detours))(lambda: start(xy_rows(both, FARTHER, 0)))
     start(z_faces(0, 1))
+    start(xz_tiles(0, FARTHER, 0))
+    start(y_faces(both, 1))
     start(x_face(both, FARTHER, 0))
-    start(xz_tiles(0, FARTHER, 0))
     start(xy_rows(both, CLOSER, 0))
     start(xz_tiles(0, CLOSER, 0))
     start(x_face(both, CLOSER, 0))
-    start(y_faces(both, 1))
+    middle = [(phase == 1) & (here[1] == gy) for gy in (1, sizes[1] - 1)]
+    for side in range(2):
+        @pl.when(middle[side])
+        def _(side=side):
+            wait_all(recv_sem.at[4], 2)
+            copy(hop.at[both, side], xyrecv.at[both, side, 0], device(FARTHER, 0, 0), 4, 0).start()
 
     def inside(x, tiles):
         return streamed(col, x, tiles, 0, False), streamed(seed, x, tiles, 1, False)
@@ -423,9 +433,8 @@
     for n, rows in ((0, 200), (1, 180), (3, 100)):
         wait_all(send_sem.at[n], rows)
 
-    @pl.when(passes_on)
-    def _():
-        wait_all(send_sem.at[4], 4)
+    pl.when(passes_on)(lambda: wait_all(send_sem.at[4], 4))
+    pl.when(middle[0] | middle[1])(lambda: wait_all(send_sem.at[4], 2))
 
     wait_all(recv_sem.at[2], 116)
     for x in (0, X - 1):
@@ -469,7 +478,7 @@
             pltpu.VMEM((3, 2, 2, 1, Z), f32),
             pltpu.VMEM((2, 2, 2, Y, Z), f32),
             pltpu.VMEM((2, 2, 2, 1, Z), f32),
-            pltpu.SemaphoreType.DMA((23,)),
+            pltpu.SemaphoreType.DMA((5,)),
             pltpu.SemaphoreType.DMA((5,)),
             pltpu.SemaphoreType.DMA((5,)),
         ],

time: 23.9 us -> 23.8 us (level)
  no operation moved by 1% of the time
where the time goes in v6:
time: 23.8 us; the launch traced here: 23.7 us
  Pallas kernels  23.1 us (97%)
  between operations  0.64 us (3%)
    pallas_call x1, Pallas kernels, body(): call(*(pltpu.with_memory_space_constraint(a, pltpu.HBM) for a in operands))  22.2 us
    pallas_call x1, Pallas kernels, body(): pl.pallas_call(store, out_shape=tuple((jax.ShapeDtypeStruct(shape, f32) f...  0.86 us

profile of v6, /device:TPU:32, one launch (start us, length us, event | category | flops | bytes accessed | tf_op | source)
XLA Modules:
  0.0 23.7 jit_solution(14153368072695828584)
XLA Ops:
  0.6 22.2 %shard_map.76 = (f32[19,8,8,128]{3,2,1,0:T(8,128)S(1)}, f32[8,8,128]{2,1,0:T(8,128)S(1)}, f32[8,8,128]{2,1,0:T(8,128)S(1)}) custom-call(f32[19,64,128]{2,1,0:T(8,128)} %bitcast.2, f32[19,64,128]{2,1,0:T(8,128)} %bitcast.3, f32[8,8,128]{2,1,0:T(8,128)} %slip_hbm.1, f32[8,8,128]{2,1,0:T(8,128)} %perm_hbm.1, s32[8,8,128]{2,1,0:T(8,128)} %kind_hbm.1), custom_call_target="tpu_custom_call" | custom-call | tf_op jit(solution)/shard_map/pallas_call | solution.py:496
  22.9 0.9 %shard_map.77 = (f32[19,8,8,128]{3,2,1,0:T(8,128)}, f32[8,8,128]{2,1,0:T(8,128)}, f32[8,8,128]{2,1,0:T(8,128)}) custom-call(f32[19,8,8,128]{3,2,1,0:T(8,128)S(1)} %get-tuple-element.6.out, f32[8,8,128]{2,1,0:T(8,128)S(1)} %get-tuple-element.7.gslip, f32[8,8,128]{2,1,0:T(8,128)S(1)} %get-tuple-element.8.gperm), custom_call_target="tpu_custom_call" | custom-call | tf_op jit(solution)/shard_map/pallas_call | solution.py:497

commit v7 on v6

--- a/solution.py
+++ b/solution.py
@@ -236,7 +236,7 @@
 
     def xy_rows(which, place, n, way=None):
         end = ends[place]
-        for side, cy in ((0, 1), (1, -1)):
+        for side, cy in ((0, 1), (1, -1)) if way is None else ((1, -1), (0, 1)):
             slot = 1 + 6 * end if cy > 0 else 2 + 4 * end
             at = BASE + (X - 1) * Y * (1 - end) + (Y - 1) * (cy > 0)
             src = fields.at[which, slot, pl.ds(at, 1), :]
@@ -397,7 +397,7 @@
         wait_all(recv_sem.at[4], 4)
         start([
             copy(hop.at[both, side], xyrecv.at[both, side, 1], device(None, cy, 0), 4, 0)
-            for side, cy in ((0, 1), (1, -1))
+            for side, cy in ((1, -1), (0, 1))
         ])
 
     wait_all(recv_sem.at[0], 200)

time: 23.8 us -> 23.8 us (level)
  no operation moved by 1% of the time
where the time goes in v7:
time: 23.8 us; the launch traced here: 23.7 us
  Pallas kernels  23.1 us (97%)
  between operations  0.64 us (3%)
    pallas_call x1, Pallas kernels, body(): call(*(pltpu.with_memory_space_constraint(a, pltpu.HBM) for a in operands))  22.2 us
    pallas_call x1, Pallas kernels, body(): pl.pallas_call(store, out_shape=tuple((jax.ShapeDtypeStruct(shape, f32) f...  0.86 us

profile of v7, /device:TPU:32, one launch (start us, length us, event | category | flops | bytes accessed | tf_op | source)
XLA Modules:
  0.0 23.7 jit_solution(4850416262955815735)
XLA Ops:
  0.6 22.2 %shard_map.76 = (f32[19,8,8,128]{3,2,1,0:T(8,128)S(1)}, f32[8,8,128]{2,1,0:T(8,128)S(1)}, f32[8,8,128]{2,1,0:T(8,128)S(1)}) custom-call(f32[19,64,128]{2,1,0:T(8,128)} %bitcast.2, f32[19,64,128]{2,1,0:T(8,128)} %bitcast.3, f32[8,8,128]{2,1,0:T(8,128)} %slip_hbm.1, f32[8,8,128]{2,1,0:T(8,128)} %perm_hbm.1, s32[8,8,128]{2,1,0:T(8,128)} %kind_hbm.1), custom_call_target="tpu_custom_call" | custom-call | tf_op jit(solution)/shard_map/pallas_call | solution.py:496
  22.9 0.9 %shard_map.77 = (f32[19,8,8,128]{3,2,1,0:T(8,128)}, f32[8,8,128]{2,1,0:T(8,128)}, f32[8,8,128]{2,1,0:T(8,128)}) custom-call(f32[19,8,8,128]{3,2,1,0:T(8,128)S(1)} %get-tuple-element.6.out, f32[8,8,128]{2,1,0:T(8,128)S(1)} %get-tuple-element.7.gslip, f32[8,8,128]{2,1,0:T(8,128)S(1)} %get-tuple-element.8.gperm), custom_call_target="tpu_custom_call" | custom-call | tf_op jit(solution)/shard_map/pallas_call | solution.py:497

commit v8 on v6

--- a/solution.py
+++ b/solution.py
@@ -182,9 +182,9 @@
                 pl.when(jnp.logical_not(spared))(functools.partial(greet, target))
             else:
                 greet(device(place, cy, cz))
+        greet(device(place, 0, 0))
         for cy, cz in SIDES[1]:
             greet(device(place, cy, cz))
-        greet(device(place, 0, 0))
     for cy in (1, -1, 0):
         for cz in (1, -1, 0):
             if cy or cz:

time: 23.8 us -> 23.8 us (level)
  no operation moved by 1% of the time
where the time goes in v8:
time: 23.8 us; the launch traced here: 23.7 us
  Pallas kernels  23.1 us (97%)
  between operations  0.64 us (3%)
    pallas_call x1, Pallas kernels, body(): call(*(pltpu.with_memory_space_constraint(a, pltpu.HBM) for a in operands))  22.2 us
    pallas_call x1, Pallas kernels, body(): pl.pallas_call(store, out_shape=tuple((jax.ShapeDtypeStruct(shape, f32) f...  0.86 us

profile of v8, /device:TPU:32, one launch (start us, length us, event | category | flops | bytes accessed | tf_op | source)
XLA Modules:
  0.0 23.7 jit_solution(13705759527794946515)
XLA Ops:
  0.6 22.2 %shard_map.76 = (f32[19,8,8,128]{3,2,1,0:T(8,128)S(1)}, f32[8,8,128]{2,1,0:T(8,128)S(1)}, f32[8,8,128]{2,1,0:T(8,128)S(1)}) custom-call(f32[19,64,128]{2,1,0:T(8,128)} %bitcast.2, f32[19,64,128]{2,1,0:T(8,128)} %bitcast.3, f32[8,8,128]{2,1,0:T(8,128)} %slip_hbm.1, f32[8,8,128]{2,1,0:T(8,128)} %perm_hbm.1, s32[8,8,128]{2,1,0:T(8,128)} %kind_hbm.1), custom_call_target="tpu_custom_call" | custom-call | tf_op jit(solution)/shard_map/pallas_call | solution.py:496
  22.8 0.9 %shard_map.77 = (f32[19,8,8,128]{3,2,1,0:T(8,128)}, f32[8,8,128]{2,1,0:T(8,128)}, f32[8,8,128]{2,1,0:T(8,128)}) custom-call(f32[19,8,8,128]{3,2,1,0:T(8,128)S(1)} %get-tuple-element.6.out, f32[8,8,128]{2,1,0:T(8,128)S(1)} %get-tuple-element.7.gslip, f32[8,8,128]{2,1,0:T(8,128)S(1)} %get-tuple-element.8.gperm), custom_call_target="tpu_custom_call" | custom-call | tf_op jit(solution)/shard_map/pallas_call | solution.py:497
